TPU v7x, 32 devices: a whole 2x2x4 slice. The times are simulated.
32 devices in a mesh: dp: 8 (over z, x), seq: 4 (over y, core).
Axes of the slice: x: 2, y: 2, z: 4, core: 2. Of those that a mesh axis runs over, the one named last changes fastest.
Arguments:
- tokens: bfloat16 [16, 1024, 1024], P(None, 'seq', 'dp'), may hold values from -6 to 6
- cotangent: bfloat16 [16, 1024, 1024], P('dp', 'seq'), may hold values from -6 to 6
- seq_lengths: int32 [16, 4], replicated, may hold values from 0 to 1024, as said below
- deal_order: int32 [16], replicated, may hold values from 0 to 15, as said below
- in_gain: bfloat16 [1024], P('dp'), may hold values from 0.5 to 1.5
- in_proj: bfloat16 [1024, 4096], P('dp'), may hold values from -0.1875 to 0.1875
- dt_proj: bfloat16 [1024, 24], P('dp'), may hold values from -0.1875 to 0.1875
- dt_bias: float32 [24], replicated, may hold values from -7 to -3
- a_log: float32 [24], replicated, may hold values from 0 to 2.5
- d_skip: float32 [24], replicated, may hold values from 0.5 to 2
- ssm_out: bfloat16 [1536, 1024], P('dp'), may hold values from -0.15625 to 0.15625
- attn_out: bfloat16 [512, 1024], P('dp'), may hold values from -1 to 1
- ffn_gain: bfloat16 [1024], P('dp'), may hold values from 0.5 to 1.5
- gate_up: bfloat16 [1024, 4096], P('dp'), may hold values from -0.1875 to 0.1875
- down_proj: bfloat16 [2048, 1024], P('dp'), may hold values from -0.125 to 0.125
Outputs:
- output: bfloat16 [16, 1024, 1024], P('dp', 'seq')
- grad_tokens: bfloat16 [16, 1024, 1024], P(None, 'seq', 'dp')
- grad_in_gain: float32 [1024], P('dp')
- grad_in_proj: float32 [1024, 4096], P('dp')
- grad_dt_proj: float32 [1024, 24], P('dp')
- grad_dt_bias: float32 [24], replicated
- grad_a_log: float32 [24], replicated
- grad_d_skip: float32 [24], replicated
- grad_ssm_out: float32 [1536, 1024], P('dp')
- grad_attn_out: float32 [512, 1024], P('dp')
- grad_ffn_gain: float32 [1024], P('dp')
- grad_gate_up: float32 [1024, 4096], P('dp')
- grad_down_proj: float32 [2048, 1024], P('dp')
Inputs may be any that keep to these rules, and one draw needn't show every extreme that they name: `seq_lengths`: row p lists the lengths of up to 4 sequences packed in order into given pack p; they sum to 1024; a zero is an unused entry; the first entry is at least 769, and some pack is one whole sequence. A permutation of the 16 packs; dealt slot j holds given pack deal_order[j]; the slots 2 * g to 2 * g + 1 belong to index g of dp.
All inputs are finite; a program needn't handle non-finite values.
Results may differ from a plain program's by a relative error of at most 0.018.
Values may be sent and summed in bfloat16 or wider, within the bound.
A program may use at most 256 MiB of HBM per device.

v0:
```python
import types

import jax
import jax.numpy as jnp
import numpy as np
from jax import lax
from jax.experimental import pallas as pl
from jax.experimental.pallas import tpu as pltpu
from jax.sharding import PartitionSpec as P

FF = 2048
QUERY_HEADS = 8
KEY_VALUE_HEADS = 2
HEAD_WIDTH = 64
MH = 24
HP = 64
NS = 128
EPS = 1e-05
THETA = 100000000000.0
BF = jnp.bfloat16
F32 = jnp.float32
CORES = 2
CHIP_HEADS = MH // CORES
XW = CHIP_HEADS * HP
QW = QUERY_HEADS // CORES * HEAD_WIDTH
Z0, X0, Q0, KV0, B0, C0, T0 = 0, XW, 2 * XW, 2 * XW + QW, 2 * XW + QW + 128, 2 * XW + QW + 256, 2 * XW + QW + 384
COLS = T0 + 128
CHUNK = 256
QB = 256
FAR = -1e30
MIB = 1 << 20
MESH = pl.DeviceIdType.MESH
VM = pltpu.VMEM


def dot(a, b, dims=((1,), (0,)), precision=None):
    return lax.dot_general(a, b, (dims, ((), ())), precision=precision, preferred_element_type=F32)


def lanes(rows, width=128):
    return lax.broadcasted_iota(jnp.int32, (rows, width), 1)


def swap_halves(v):
    low = lanes(v.shape[0], v.shape[1]) % 64 < 32
    return jnp.where(low, pltpu.roll(v, v.shape[1] - 32, 1), pltpu.roll(v, 32, 1))


def turn(v, cosine, sine):
    return v * cosine + swap_halves(v) * sine


def turn_back(v, cosine, sine):
    return v * cosine - swap_halves(v) * sine


def widen(v, spread):
    v = jnp.where(lanes(v.shape[0]) < 64, v, 0.0)
    top = v.astype(BF)
    rest = (v - top.astype(F32)).astype(BF).astype(F32)
    both = top.astype(F32) + pltpu.roll(rest, 64, 1)
    return dot(both.astype(BF), spread)


def attn_masks(segc_ref, segr_ref, i, upto):
    rows = pl.ds(i * QB, QB)
    same = segc_ref[rows, 0:1] == segr_ref[0:1, 0:upto]
    t = lax.broadcasted_iota(jnp.int32, (QB, upto), 0) + i * QB
    u = lax.broadcasted_iota(jnp.int32, (QB, upto), 1)
    return jnp.where(same & (u <= t), 0.0, FAR)


def key_value_pairs(kv, cosine, sine):
    low = lanes(kv.shape[0]) < 64
    other = pltpu.roll(kv, 64, 1)
    kk = turn(jnp.where(low, kv, other), cosine, sine)
    vv = jnp.where(low, other, kv)
    return kk.astype(BF), vv.astype(BF)


def attention_forward(proj_ref, cos_ref, sin_ref, segc_ref, segr_ref, attn_ref, lse_ref, tick):
    seq_len = proj_ref.shape[0]
    kk, vv = key_value_pairs(proj_ref[:, KV0 : KV0 + 128].astype(F32), cos_ref[...], sin_ref[...])
    low = lanes(QB) < 64
    for i in range(seq_len // QB):
        rows = slice(i * QB, (i + 1) * QB)
        upto = (i + 1) * QB
        mask = attn_masks(segc_ref, segr_ref, i, upto)
        tops = jnp.zeros((QB, 128), F32)
        for pair in range(QW // 128):
            q = proj_ref[rows, Q0 + 128 * pair : Q0 + 128 * (pair + 1)].astype(F32)
            q = turn(q, cos_ref[rows, :], sin_ref[rows, :]) * HEAD_WIDTH**-0.5
            outs = []
            for half in range(2):
                qh = jnp.where(low if half == 0 else ~low, q, 0.0).astype(BF)
                s = dot(qh, kk[:upto], ((1,), (1,))) + mask
                top = jnp.max(s, axis=1, keepdims=True)
                e = jnp.exp(s - top)
                total = jnp.sum(e, axis=1, keepdims=True)
                outs.append(dot(e.astype(BF), vv[:upto]) / total)
                tops = jnp.where(lanes(QB) == 2 * pair + half, top + jnp.log(total), tops)
                tick()
            attn_ref[rows, 128 * pair : 128 * (pair + 1)] = jnp.where(low, outs[0], outs[1]).astype(BF)
        lse_ref[rows, :] = tops


def attention_backward(proj_ref, cos_ref, sin_ref, segc_ref, segr_ref, attn_ref, lse_ref, gattn_ref, gproj_ref, gkv, tick):
    seq_len = proj_ref.shape[0]
    kk, vv = key_value_pairs(proj_ref[:, KV0 : KV0 + 128].astype(F32), cos_ref[...], sin_ref[...])
    low = lanes(QB) < 64
    gkv[...] = jnp.zeros_like(gkv)
    pick = (lax.broadcasted_iota(jnp.int32, (QW, 128), 0) // 64 == lanes(QW)).astype(BF)
    for i in range(seq_len // QB):
        rows = slice(i * QB, (i + 1) * QB)
        upto = (i + 1) * QB
        same = segc_ref[0:upto, 0:1] == segr_ref[0:1, rows]
        t = lanes(upto, QB) + i * QB
        u = lax.broadcasted_iota(jnp.int32, (upto, QB), 0)
        mask = jnp.where(same & (u <= t), 0.0, FAR)
        weighed = gattn_ref[rows, :].astype(F32) * attn_ref[rows, :].astype(F32)
        deltas = dot(weighed.astype(BF), pick).T
        tops = lse_ref[rows, :].T
        for pair in range(QW // 128):
            cosine, sine = cos_ref[rows, :], sin_ref[rows, :]
            q = proj_ref[rows, Q0 + 128 * pair : Q0 + 128 * (pair + 1)].astype(F32)
            q = turn(q, cosine, sine) * HEAD_WIDTH**-0.5
            g = gattn_ref[rows, 128 * pair : 128 * (pair + 1)]
            grads = []
            for half in range(2):
                head = 2 * pair + half
                mine = low if half == 0 else ~low
                qh = jnp.where(mine, q, 0.0).astype(BF)
                gh = jnp.where(mine, g, jnp.zeros_like(g))
                s = dot(kk[:upto], qh, ((1,), (1,))) + mask
                p = jnp.exp(s - tops[head : head + 1, :])
                gp = dot(vv[:upto], gh, ((1,), (1,)))
                gs = (p * (gp - deltas[head : head + 1, :])).astype(BF)
                gkv[0:upto, 0:128] += dot(gs, qh)
                gkv[0:upto, 128:256] += dot(p.astype(BF), gh)
                grads.append(dot(gs, kk[:upto], ((0,), (0,))))
                tick()
            gq = jnp.where(low, grads[0], grads[1]) * HEAD_WIDTH**-0.5
            gproj_ref[rows, Q0 + 128 * pair : Q0 + 128 * (pair + 1)] = turn_back(gq, cosine, sine).astype(BF)
    gk = gkv[:, 0:128]
    gv = gkv[:, 128:256]
    gk = turn_back(gk + pltpu.roll(gk, 64, 1), cos_ref[...], sin_ref[...])
    gv = gv + pltpu.roll(gv, 64, 1)
    gproj_ref[:, KV0 : KV0 + 128] = jnp.where(lanes(seq_len) < 64, gk, gv).astype(BF)


def scan_pieces(j, proj_ref, segc_ref, segr_ref, par_ref):
    rows = pl.ds(j * CHUNK, CHUNK)
    seg = segc_ref[rows, :]
    prev = segc_ref[pl.ds(j * CHUNK - 1, 1), :] if j else jnp.full((1, 128), -1, jnp.int32)
    last = segc_ref[pl.ds(j * CHUNK + CHUNK - 1, 1), :]
    valid = lanes(CHUNK) < CHIP_HEADS
    raw = proj_ref[rows, T0 : T0 + 128].astype(F32) + par_ref[0:1, :]
    dt = jnp.where(valid, jnp.maximum(raw, 0.0) + jnp.log1p(jnp.exp(-jnp.abs(raw))), 0.0)
    decay = dt * par_ref[1:2, :]
    place = lax.broadcasted_iota(jnp.int32, (CHUNK, CHUNK), 0)
    under = (place >= lanes(CHUNK, CHUNK)).astype(F32)
    cum = dot(under, decay, precision=lax.Precision.HIGHEST)
    end = cum[CHUNK - 1 : CHUNK, :]
    from_start = jnp.where(seg == prev, jnp.exp(cum), 0.0)
    to_end = jnp.where(seg == last, jnp.exp(end - cum), 0.0)
    keep = jnp.where(last == prev, jnp.exp(end), 0.0)
    return rows, raw, dt, decay, cum, from_start, to_end, keep, under


def scan_forward(proj_ref, segc_ref, segr_ref, par_ref, spread_ref, wide_ref, gated_ref, y_ref, states_ref, state, tick):
    spread = spread_ref[...]
    state[...] = jnp.zeros_like(state)

    for j in range(proj_ref.shape[0] // CHUNK):
        rows, raw, dt, decay, cum, from_start, to_end, keep, under = scan_pieces(j, proj_ref, segc_ref, segr_ref, par_ref)
        place = lax.broadcasted_iota(jnp.int32, (CHUNK, CHUNK), 0)
        same = segc_ref[rows, 0:1] == segr_ref[0:1, rows]
        mask = jnp.where(same & (place >= lanes(CHUNK, CHUNK)), 0.0, FAR)
        cum_t = cum.T
        b = proj_ref[rows, B0 : B0 + 128]
        c = proj_ref[rows, C0 : C0 + 128]
        cb = dot(c, b, ((1,), (1,)))
        x = proj_ref[rows, X0 : X0 + XW].astype(F32)
        xdt = x * widen(dt, spread)
        xdt_low = xdt.astype(BF)
        old = state[...]
        states_ref[j] = old
        y_state = dot(c, old.astype(BF)) * widen(from_start, spread)
        low = lanes(CHUNK) < 64
        for pair in range(CHIP_HEADS // 2):
            cols = slice(128 * pair, 128 * (pair + 1))
            xp = xdt_low[:, cols]
            local = y_state[:, cols]
            for half in range(2):
                h = 2 * pair + half
                spread_h = jnp.exp(cum[:, h : h + 1] - cum_t[h : h + 1, :] + mask)
                mix = (cb * spread_h).astype(BF)
                xh = jnp.where(low if half == 0 else ~low, xp, jnp.zeros_like(xp))
                local = local + dot(mix, xh)
            y_ref[rows, cols] = local
            y = (local + x[:, cols] * wide_ref[0:1, cols]).astype(BF).astype(F32)
            z = proj_ref[rows, Z0 + 128 * pair : Z0 + 128 * (pair + 1)].astype(F32)
            gated_ref[rows, cols] = (y * (z / (1.0 + jnp.exp(-z)))).astype(BF)
            tick()
        weighted = (xdt * widen(to_end, spread)).astype(BF)
        keep_wide = widen(jnp.broadcast_to(keep, (8, 128)), spread)[0:1, :]
        state[...] = old * keep_wide + dot(b, weighted, ((0,), (0,)))


def gate_backward(proj_ref, wide_ref, y_ref, ggated_ref, gproj_ref, gy_ref, tick):
    for j in range(proj_ref.shape[0] // CHUNK):
        rows = pl.ds(j * CHUNK, CHUNK)
        x = proj_ref[rows, X0 : X0 + XW].astype(F32)
        z = proj_ref[rows, Z0 : Z0 + XW].astype(F32)
        gg = ggated_ref[rows, :].astype(F32)
        y = (y_ref[rows, :] + x * wide_ref[0:1, :]).astype(BF).astype(F32)
        sig = 1.0 / (1.0 + jnp.exp(-z))
        gy_ref[rows, :] = (gg * (z * sig)).astype(BF)
        gproj_ref[rows, Z0 : Z0 + XW] = (gg * y * (sig * (1.0 + z * (1.0 - sig)))).astype(BF)
        tick()


def scan_backward(proj_ref, segc_ref, segr_ref, par_ref, spread_ref, wide_ref, y_ref, states_ref, gy_ref, gproj_ref, gpar_ref, gstate, tick):
    spread = spread_ref[...]
    gstate[...] = jnp.zeros_like(gstate)
    gpar_ref[...] = jnp.zeros_like(gpar_ref)
    chunks = proj_ref.shape[0] // CHUNK

    def narrow(v):
        top = v.astype(BF)
        rest = (v - top.astype(F32)).astype(BF)
        return dot(top, spread, ((1,), (1,))) + dot(rest, spread, ((1,), (1,)))

    for j in reversed(range(chunks)):
        rows, raw, dt, decay, cum, from_start, to_end, keep, under = scan_pieces(j, proj_ref, segc_ref, segr_ref, par_ref)
        place = lax.broadcasted_iota(jnp.int32, (CHUNK, CHUNK), 0)
        same = segc_ref[rows, 0:1] == segr_ref[0:1, rows]
        mask = jnp.where(same & (place <= lanes(CHUNK, CHUNK)), 0.0, FAR)
        cum_t = cum.T
        b = proj_ref[rows, B0 : B0 + 128]
        c = proj_ref[rows, C0 : C0 + 128]
        bc = dot(b, c, ((1,), (1,)))
        x = proj_ref[rows, X0 : X0 + XW].astype(F32)
        dt_wide = widen(dt, spread)
        xdt_low = (x * dt_wide).astype(BF)
        start_wide = widen(from_start, spread)
        end_wide = widen(to_end, spread)
        old = states_ref[j]
        gnew = gstate[...]
        y_own = y_ref[rows, :]
        gy_low = gy_ref[rows, :]
        gy = gy_low.astype(F32)
        gx_state = end_wide * dot(b, gnew.astype(BF))
        gbc = jnp.zeros((CHUNK, CHUNK), F32)
        low = lanes(CHUNK) < 64
        gxdt = []
        for pair in range(CHIP_HEADS // 2):
            cols = slice(128 * pair, 128 * (pair + 1))
            xp, gp = xdt_low[:, cols], gy_low[:, cols]
            total = gx_state[:, cols]
            for half in range(2):
                h = 2 * pair + half
                mine = low if half == 0 else ~low
                spread_h = jnp.exp(cum_t[h : h + 1, :] - cum[:, h : h + 1] + mask)
                mix = (bc * spread_h).astype(BF)
                gh = jnp.where(mine, gp, jnp.zeros_like(gp))
                total = total + dot(mix, gh)
                gbc = gbc + dot(xp, gh, ((1,), (1,))) * spread_h
            gxdt.append(total)
            tick()
        gxdt = jnp.concatenate(gxdt, axis=1)
        gstart = (gy * start_wide).astype(BF)
        weighted = (xdt_low.astype(F32) * end_wide).astype(BF)
        gbc_low = gbc.astype(BF)
        gnew_low, old_low = gnew.astype(BF), old.astype(BF)
        gproj_ref[rows, C0 : C0 + 128] = (dot(gbc_low, b, ((0,), (0,))) + dot(gstart, old_low, ((1,), (1,)))).astype(BF)
        gproj_ref[rows, B0 : B0 + 128] = (dot(gbc_low, c) + dot(weighted, gnew_low, ((1,), (1,)))).astype(BF)
        keep_wide = widen(jnp.broadcast_to(keep, (8, 128)), spread)[0:1, :]
        kept = jnp.sum(old * gnew, axis=0, keepdims=True) * keep_wide
        gstate[...] = gnew * keep_wide + dot(c, gstart, ((0,), (0,)))
        xdt_f = xdt_low.astype(F32)
        gcum = narrow(gy * y_own) - narrow(xdt_f * gxdt)
        at_end = jnp.sum(xdt_f * gx_state, axis=0, keepdims=True) + kept
        at_end = narrow(jnp.broadcast_to(at_end, (8, XW)))[0:1, :]
        gdecay = dot(under, gcum, ((0,), (0,)), precision=lax.Precision.HIGHEST) + at_end
        gdt = narrow(gxdt * x) + gdecay * par_ref[1:2, :]
        graw = gdt / (1.0 + jnp.exp(-raw))
        graw = jnp.where(lanes(CHUNK) < CHIP_HEADS, graw, 0.0)
        gproj_ref[rows, T0 : T0 + 128] = graw.astype(BF)
        gproj_ref[rows, X0 : X0 + XW] = (gxdt * dt_wide + gy * wide_ref[0:1, :]).astype(BF)
        gpar_ref[0:1, :] += jnp.sum(graw, axis=0, keepdims=True)
        gpar_ref[1:2, :] += jnp.sum(gdecay * decay, axis=0, keepdims=True)
        skip = jnp.sum(gy * x, axis=0, keepdims=True)
        gpar_ref[2:3, :] += narrow(jnp.broadcast_to(skip, (8, XW)))[0:1, :]


class Ticker:
    def __init__(self, steps, ticks=1):
        self.steps, self.done = steps, 0
        self.plan(len(steps), ticks)

    def plan(self, count, ticks):
        self.first, self.last = self.done, min(self.done + count, len(self.steps))
        self.ticks, self.calls = ticks, 0

    def run(self, upto):
        while self.done < upto:
            if not isinstance(self.steps[self.done], int):
                self.steps[self.done]()
            self.done += 1

    def __call__(self):
        self.calls = min(self.calls + 1, self.ticks)
        self.run(self.first + (self.last - self.first) * self.calls // self.ticks)

    def reach(self, mark):
        if mark in self.steps[self.done :]:
            self.run(self.steps.index(mark) + 1)

    def drain(self):
        self.run(len(self.steps))


def whole(n):
    return [pl.BlockSpec(memory_space=VM)] * n


def place():
    d, s = lax.axis_index("dp"), lax.axis_index("seq")
    return d // 2, d % 2, s // 2, s % 2


def device(z, x, y, c):
    return (2 * z + x, 2 * y + c)


def greet(peers):
    barrier = pltpu.get_barrier_semaphore()
    for peer in peers:
        pl.semaphore_signal(barrier, inc=1, device_id=peer, device_id_type=MESH)
    pl.semaphore_wait(barrier, len(peers))


def send(src, dst, sems, k, target):
    copy = pltpu.make_async_remote_copy(
        src_ref=src, dst_ref=dst, send_sem=sems[0].at[k], recv_sem=sems[1].at[k], device_id=target, device_id_type=MESH
    )
    copy.start()
    return copy


def landed(dst, sems, k, target):
    pltpu.make_async_remote_copy(
        src_ref=dst, dst_ref=dst, send_sem=sems[0].at[k], recv_sem=sems[1].at[k], device_id=target, device_id_type=MESH
    ).wait_recv()


ARRAY_SENDS = 14
CORNER_X = 3
W_CUTS = 3


class Gather:
    def __init__(self, src, dst, sems, base, local_sem):
        self.src, self.dst, self.sems, self.base = src, dst, sems, base
        self.local_sem = local_sem
        self.z, self.x, self.y, self.c = place()
        half = src.shape[0] // 2
        self.mine = pl.ds(self.y * half, half)
        self.other = pl.ds((1 - self.y) * half, half)
        self.sent, self.sent_inner = [], []
        self.inner = (self.z == 1) | (self.z == 2)
        self.xpeer = device(self.z, 1 - self.x, self.y, self.c)
        self.ypeer = device(self.z, self.x, 1 - self.y, self.c)

    def push_inner(self, k, src, dst, target):
        def copy():
            return pltpu.make_async_remote_copy(
                src_ref=src,
                dst_ref=dst,
                send_sem=self.sems[0].at[self.base + k],
                recv_sem=self.sems[1].at[self.base + 2],
                device_id=target,
                device_id_type=MESH,
            )

        pl.when(self.inner)(lambda: copy().start())
        self.sent_inner.append(copy)

    def block(self, r, x, rows):
        return self.dst.at[2 * (self.z ^ r) + x, rows]

    def push(self, k, ref, target, dst=None):
        self.sent.append(send(ref, ref if dst is None else dst, self.sems, self.base + k, target))

    def start(self):
        own = 2 * self.z + self.x
        self.local = pltpu.make_async_copy(self.src, self.dst.at[own], self.local_sem)
        self.local.start()
        for r in (1, 2):
            target = device(self.z ^ r, self.x, self.y, self.c)
            self.push(r - 1, self.src.at[self.mine], target, self.dst.at[own, self.mine])
        target = device(self.z ^ 3, self.x, self.y, self.c)
        self.push_inner(2, self.src.at[self.mine], self.dst.at[own, self.mine], target)
        self.push(3, self.src, self.xpeer, self.dst.at[own])

    def cross(self):
        landed(self.block(0, 1 - self.x, slice(None)), self.sems, self.base + 3, self.xpeer)
        self.push(4, self.block(0, 1 - self.x, self.mine), device(self.z ^ 1, self.x, self.y, self.c))

    def forward(self, r):
        ref = self.block(r, self.x, self.mine)
        landed(ref, self.sems, self.base + r - 1, self.xpeer)
        if r == 2:
            self.push_inner(13, ref, ref, device(self.z ^ 1, self.x, self.y, self.c))
        self.push(6 + r, ref, self.ypeer)
        if r > 1:
            self.push(3 + r, ref, self.xpeer)

    def corner(self, r):
        if r == CORNER_X:
            ref = self.block(r, self.x, self.other)
            landed(ref, self.sems, self.base + 6 + r, self.ypeer)
            self.push(9 + r, ref, self.xpeer)
        else:
            ref = self.block(r, 1 - self.x, self.mine)
            landed(ref, self.sems, self.base + 3 + r, self.xpeer)
            self.push(9 + r, ref, self.ypeer)

    def arrive(self):
        for r in (1, 2, 3):
            if r == CORNER_X:
                landed(self.block(r, 1 - self.x, self.mine), self.sems, self.base + 3 + r, self.xpeer)
            else:
                landed(self.block(r, self.x, self.other), self.sems, self.base + 6 + r, self.ypeer)
            landed(self.block(r, 1 - self.x, self.other), self.sems, self.base + 9 + r, self.ypeer)
        self.local.wait()

    def finish(self):
        for copy in self.sent:
            copy.wait_send()
        for copy in self.sent_inner:
            pl.when(self.inner)(lambda copy=copy: copy().wait_send())


def gather_steps(gathers):
    def one(g):
        return [
            lambda: g.forward(1),
            g.cross,
            lambda: g.forward(2),
            lambda: g.forward(3),
        ]

    def corners(g):
        return [lambda r=r: g.corner(r) for r in (2, 3, 1)]

    steps = []
    count = len(gathers)
    for k in range(count + 1):
        if k + 2 < count:
            steps.append(gathers[k + 2].start)
        steps += one(gathers[k]) if k < count else []
        steps += corners(gathers[k - 1]) + [k - 1] if k else []
    return steps


def reduce_steps(sums, partner):
    def early(s):
        return [
            s.cross,
            lambda: s.relay(2),
            lambda: s.root(1),
            lambda: s.relay(3),
            lambda: s.relay(0),
        ]

    def late(s):
        return [lambda r=r: s.root(r) for r in (2, 3, 0)]

    steps = []
    count = len(sums)
    for k in range(count + 3):
        if k < count:
            steps += early(sums[k])
        if 0 <= k - 1 < count:
            steps += late(sums[k - 1])
        if 0 <= k - 2 < count:
            steps.append(lambda s=sums[k - 2]: s.total(partner))
        if 0 <= k - 3 < count:
            steps.append(lambda s=sums[k - 3]: s.spread(partner))
    return steps


def chip_peers():
    z, x, y, c = place()
    peers = [device(z ^ r, x, y, c) for r in (1, 2, 3)]
    peers += [device(z, 1 - x, y, c), device(z, x, 1 - y, c), device(z, x, y, 1 - c)]
    return peers


def start_kernel(dealt, in_proj, beside, rows, weights, w, kv, dsend, drecv, wsend, wrecv, local):
    z, x, y, c = place()
    own = 2 * z + x
    slot = 2 * y + c
    partner = device(z, x, y, 1 - c)
    others = [(r, i, j) for r in range(4) for i in range(2) for j in range(2) if r or i or j]
    targets = [device(z ^ r, x ^ i, y ^ j, c) for r, i, j in others]
    lane = lambda start, size: pl.ds(pl.multiple_of(start, 128), size)
    inner = MH * HP
    q_start = 2 * inner + 2 * NS
    kv_start = q_start + QUERY_HEADS * HEAD_WIDTH
    pieces = [
        (lane(XW * c, XW), w.at[:, Z0 : Z0 + XW]),
        (lane(inner + XW * c, XW), w.at[:, X0 : X0 + XW]),
        (lane(q_start + QW * c, QW), w.at[:, Q0 : Q0 + QW]),
        (lane(2 * inner, 2 * NS), w.at[:, B0 : B0 + 2 * NS]),
        (lane(kv_start, 256), kv),
    ]
    copies = [pltpu.make_async_copy(in_proj.at[:, cols], dst, local.at[2 + i]) for i, (cols, dst) in enumerate(pieces)]
    for copy in copies:
        copy.start()
    barrier = pltpu.get_barrier_semaphore()
    for peer in targets + [partner]:
        pl.semaphore_signal(barrier, inc=1, device_id=peer, device_id_type=MESH)
    first = c == 0
    lane_of = lanes(w.shape[0])
    near = beside[...].astype(F32).T
    far = pltpu.roll(near, 128 - CHIP_HEADS, 1)
    tail = jnp.where(lane_of < CHIP_HEADS, jnp.where(first, near, far), jnp.where(lane_of < CHIP_HEADS + 2, far, 0.0))
    w[:, T0 : T0 + 128] = tail.astype(BF)
    for copy in copies:
        copy.wait()
    keys, values = kv[:, :128].astype(F32), kv[:, 128:].astype(F32)
    keys = jnp.where(first, keys, pltpu.roll(keys, 64, 1))
    values = jnp.where(first, pltpu.roll(values, 64, 1), values)
    w[:, KV0 : KV0 + 128] = jnp.where(lane_of < 64, keys, values).astype(BF)
    pl.semaphore_wait(barrier, len(targets) + 1)
    sems = (dsend, drecv)
    cuts = [slice(i * COLS // W_CUTS, (i + 1) * COLS // W_CUTS) for i in range(W_CUTS)]
    gathers = [
        Gather(w.at[:, cols], weights.at[:, :, cols], (wsend, wrecv), ARRAY_SENDS * i, local.at[7 + i])
        for i, cols in enumerate(cuts)
    ]
    columns = lambda d: lane(d * 128, 128)
    sent = []
    for gather in gathers[:2]:
        gather.start()
    for k, (r, i, j) in enumerate(others):
        pack = 2 * (2 * (z ^ r) + (x ^ i)) + (y ^ j)
        sent.append(send(dealt.at[pack], rows.at[slot, :, columns(own)], sems, k, targets[k]))
    here = pltpu.make_async_copy(dealt.at[2 * own + y], rows.at[slot, :, columns(own)], local.at[1])
    here.start()
    for step in gather_steps(gathers):
        if not isinstance(step, int):
            step()
    here.wait()
    for same_y in (True, False):
        for k, (r, i, j) in enumerate(others):
            if (j == 0) == same_y:
                src = 2 * (z ^ r) + (x ^ i)
                landed(rows.at[2 * (y ^ j) + c, :, columns(src)], sems, k, targets[k])
        ref = rows.at[slot if same_y else 2 * (1 - y) + c]
        sent.append(send(ref, ref, sems, 15 if same_y else 16, partner))
    landed(rows.at[2 * y + 1 - c], sems, 15, partner)
    landed(rows.at[2 * (1 - y) + 1 - c], sems, 16, partner)
    for gather in gathers:
        gather.arrive()
    for copy in sent:
        copy.wait_send()
    for gather in gathers:
        gather.finish()


def start_transfers(dealt, in_proj, beside):
    packs, span, width = dealt.shape
    block = in_proj.shape[0]
    return pl.pallas_call(
        start_kernel,
        name="deal_and_gather",
        out_shape=(
            jax.ShapeDtypeStruct((4, span, 8 * width), BF),
            jax.ShapeDtypeStruct((8, block, COLS), BF),
        ),
        in_specs=whole(1) + any_specs(1) + whole(1),
        out_specs=tuple(any_specs(2)),
        scratch_shapes=[
            VM((block, COLS), BF),
            VM((block, 256), BF),
            pltpu.SemaphoreType.DMA((17,)),
            pltpu.SemaphoreType.DMA((17,)),
            pltpu.SemaphoreType.DMA((W_CUTS * ARRAY_SENDS,)),
            pltpu.SemaphoreType.DMA((W_CUTS * ARRAY_SENDS,)),
            pltpu.SemaphoreType.DMA((7 + W_CUTS,)),
        ],
        compiler_params=pltpu.CompilerParams(collective_id=0, has_side_effects=True),
    )(dealt, in_proj, beside)


def any_specs(n):
    return [pl.BlockSpec(memory_space=pl.ANY)] * n


class Cotangents:
    def __init__(self, src, dst, sems, local_sem):
        self.src, self.dst, self.sems, self.local_sem = src, dst, sems, local_sem
        self.z, self.x, self.y, self.c = place()
        self.slot = 2 * self.y + self.c
        self.partner = device(self.z, self.x, self.y, 1 - self.c)
        self.ypeer = device(self.z, self.x, 1 - self.y, self.c)

    def start(self):
        src, dst = self.src, self.dst
        self.sent = [
            send(src.at[1 - self.y], dst.at[self.slot], self.sems, 0, self.ypeer),
            send(src.at[self.y], dst.at[self.slot], self.sems, 1, self.partner),
        ]
        self.local = pltpu.make_async_copy(src.at[self.y], dst.at[self.slot], self.local_sem)
        self.local.start()

    def forward(self):
        ref = self.dst.at[2 * (1 - self.y) + self.c]
        landed(ref, self.sems, 0, self.ypeer)
        self.sent.append(send(ref, ref, self.sems, 2, self.partner))

    def arrive(self):
        landed(self.dst.at[2 * self.y + 1 - self.c], self.sems, 1, self.partner)
        landed(self.dst.at[2 * (1 - self.y) + 1 - self.c], self.sems, 2, self.partner)
        self.local.wait()

    def finish(self):
        for copy in self.sent:
            copy.wait_send()


class Halves:
    def __init__(self, gather, dst, sems, base, local_sem):
        self.gather, self.dst, self.sems, self.base, self.local_sem = gather, dst, sems, base, local_sem
        z, x, y, self.c = place()
        self.partner = device(z, x, y, 1 - self.c)

    def columns(self, k):
        half = self.gather.src.shape[1]
        return self.dst.at[:, :, pl.ds(pl.multiple_of(k * half, 128), half)]

    def start(self):
        src, c = self.gather.dst, self.c
        self.gather.arrive()
        self.local = pltpu.make_async_copy(src.at[pl.ds(4 * c, 4)], self.columns(c), self.local_sem)
        self.local.start()
        self.sent = send(src.at[pl.ds(4 * (1 - c), 4)], self.columns(c), self.sems, self.base, self.partner)

    def arrive(self):
        landed(self.columns(1 - self.c), self.sems, self.base, self.partner)
        self.local.wait()
        self.sent.wait_send()


def plain_forward_kernel(proj, cosine, sine, segc, segr, par, spread, wide, gated, attn, lse, y_own, states, state):
    tick = Ticker([])
    attention_forward(proj, cosine, sine, segc, segr, attn, lse, tick)
    scan_forward(proj, segc, segr, par, spread, wide, gated, y_own, states, state, tick)


def mixer_forward(proj, consts):
    seq_len = proj.shape[0]
    return pl.pallas_call(
        plain_forward_kernel,
        name="mixer_forward",
        out_shape=(
            jax.ShapeDtypeStruct((seq_len, XW), BF),
            jax.ShapeDtypeStruct((seq_len, QW), BF),
            jax.ShapeDtypeStruct((seq_len, 128), F32),
            jax.ShapeDtypeStruct((seq_len, XW), F32),
            jax.ShapeDtypeStruct((seq_len // CHUNK, NS, XW), F32),
        ),
        in_specs=whole(8),
        out_specs=tuple(whole(5)),
        scratch_shapes=[VM((NS, XW), F32)],
        compiler_params=pltpu.CompilerParams(vmem_limit_bytes=56 * MIB),
    )(proj, *consts)


class Reduce:
    def __init__(self, part, out, far, near_x, near_y, deep, sems, base):
        self.part, self.out, self.far, self.near_x, self.near_y, self.deep = part, out, far, near_x, near_y, deep
        self.sems, self.base = sems, base
        self.z, self.x, self.y, self.c = place()
        half = part.shape[1] // 2
        self.mine = pl.ds(self.y * half, half)
        self.other = pl.ds((1 - self.y) * half, half)
        self.xpeer = device(self.z, 1 - self.x, self.y, self.c)
        self.ypeer = device(self.z, self.x, 1 - self.y, self.c)
        self.sent = []

    def piece(self, r, x, rows):
        return self.part.at[2 * (self.z ^ r) + x, rows]

    def push(self, k, src, dst, target):
        self.sent.append(send(src, dst, self.sems, self.base + k, target))

    def start(self):
        zpeer = device(self.z ^ 1, self.x, self.y, self.c)
        self.push(5, self.piece(1, 1 - self.x, self.mine), self.near_x.at[1], zpeer)
        self.push(1, self.piece(1, 1 - self.x, self.other), self.far.at[1], zpeer)
        for r in (2, 3):
            far = self.piece(r, 1 - self.x, self.other)
            self.push(r, far, self.far.at[r], self.ypeer if r == 2 else self.xpeer)
        self.push(9, self.piece(1, self.x, self.other), self.near_y.at[1], self.ypeer)

    def add(self, ref, r, own):
        ref[r] = (own[...].astype(F32) + ref[r].astype(F32)).astype(BF)

    def cross(self):
        landed(self.far.at[1], self.sems, self.base + 1, self.xpeer)
        self.add(self.far, 1, self.piece(0, 1 - self.x, self.other))
        self.push(0, self.far.at[1], self.far.at[0], self.xpeer)
        landed(self.near_x.at[1], self.sems, self.base + 5, self.xpeer)
        self.add(self.near_x, 1, self.piece(0, 1 - self.x, self.mine))
        self.push(4, self.near_x.at[1], self.near_x.at[0], self.xpeer)

    def relay(self, r):
        landed(self.far.at[r], self.sems, self.base + r, self.xpeer)
        if r == 2:
            self.add(self.far, r, self.piece(r, 1 - self.x, self.mine))
            self.push(4 + r, self.far.at[r], self.near_x.at[r], self.xpeer)
            self.push(8 + r, self.piece(r, self.x, self.other), self.near_y.at[r], self.ypeer)
            return
        self.add(self.far, r, self.piece(r, self.x, self.other))
        self.push(8 + r, self.far.at[r], self.near_y.at[r], self.ypeer)
        if r:
            self.push(4 + r, self.piece(r, 1 - self.x, self.mine), self.near_x.at[r], self.xpeer)

    def root(self, r):
        landed(self.near_y.at[r], self.sems, self.base + 8 + r, self.ypeer)
        total = self.piece(r, self.x, self.mine)[...].astype(F32) + self.near_y[r].astype(F32)
        if r != 1:
            landed(self.near_x.at[r], self.sems, self.base + 4 + r, self.xpeer)
            total = total + self.near_x[r].astype(F32)
        self.near_y[r] = total.astype(BF)
        if r:
            target = device(self.z ^ r, self.x, self.y, self.c)
            self.push(11 + r, self.near_y.at[r], self.deep.at[r - 1], target)

    def total(self, partner):
        for r in (1, 2, 3):
            landed(self.deep.at[r - 1], self.sems, self.base + 11 + r, self.xpeer)
        total = self.near_y[0].astype(F32) + self.deep[0].astype(F32)
        total = total + (self.deep[1].astype(F32) + self.deep[2].astype(F32))
        self.out[self.c, self.mine] = total.astype(BF)
        ref = self.out.at[self.c, self.mine]
        self.push(15, ref, ref, self.ypeer)
        self.push(16, ref, ref, partner)

    def spread(self, partner):
        ref = self.out.at[self.c, self.other]
        landed(ref, self.sems, self.base + 15, self.ypeer)
        self.push(17, ref, ref, partner)

    def finish(self, partner):
        landed(self.out.at[1 - self.c, self.mine], self.sems, self.base + 16, partner)
        landed(self.out.at[1 - self.c, self.other], self.sems, self.base + 17, partner)
        for copy in self.sent:
            copy.wait_send()


REDUCE_SENDS = 18


def reduce_buffers(parts):
    scratch = []
    for p in parts:
        half = (p.shape[1] // 2, p.shape[2])
        scratch += [VM((4,) + half, BF)] * 3 + [VM((3,) + half, BF)]
    total = REDUCE_SENDS * len(parts)
    return scratch + [pltpu.SemaphoreType.DMA((total,))] * 2


def plain_backward_kernel(proj, cosine, sine, segc, segr, par, spread, wide, attn, lse, y_own, states, ggated, gattn, gproj, gpar, gkv, gstate, gy):
    tick = Ticker([])
    gate_backward(proj, wide, y_own, ggated, gproj, gy, tick)
    attention_backward(proj, cosine, sine, segc, segr, attn, lse, gattn, gproj, gkv, tick)
    scan_backward(proj, segc, segr, par, spread, wide, y_own, states, gy, gproj, gpar, gstate, tick)


def mixer_backward(proj, consts, saved, ggated, gattn):
    seq_len = proj.shape[0]
    return pl.pallas_call(
        plain_backward_kernel,
        name="mixer_backward",
        out_shape=(
            jax.ShapeDtypeStruct((seq_len, COLS), BF),
            jax.ShapeDtypeStruct((8, 128), F32),
        ),
        in_specs=whole(14),
        out_specs=tuple(whole(2)),
        scratch_shapes=[VM((seq_len, 256), F32), VM((NS, XW), F32), VM((seq_len, XW), BF)],
        compiler_params=pltpu.CompilerParams(vmem_limit_bytes=56 * MIB),
    )(proj, *consts, *saved, ggated, gattn)


class Mover:
    def __init__(self, sems):
        self.sems, self.used, self.loads, self.stores = sems, 0, {}, []

    def copy(self, src, dst):
        copy = pltpu.make_async_copy(src, dst, self.sems.at[self.used])
        self.used += 1
        copy.start()
        return copy

    def load(self, src, dst):
        self.loads.setdefault(id(dst), []).append(self.copy(src, dst))

    def need(self, *refs):
        for ref in refs:
            for copy in self.loads.pop(id(ref), []):
                copy.wait()

    def store(self, src, dst):
        copy = self.copy(src, dst)
        self.stores.append(copy)
        return copy

    def flush(self):
        for copies in self.loads.values():
            for copy in copies:
                copy.wait()
        for copy in self.stores:
            copy.wait()


def shape(dims, dtype=BF):
    return jax.ShapeDtypeStruct(tuple(dims), dtype)


def fused_call(kernel, name, inputs, outputs, scratch, spaces, collective_id):
    names = list(inputs) + list(outputs) + list(scratch)

    def wrapped(*refs):
        kernel(types.SimpleNamespace(**dict(zip(names, refs))))

    place_of = lambda n: pl.BlockSpec(memory_space=spaces.get(n, pl.ANY))
    outs = pl.pallas_call(
        wrapped,
        name=name,
        out_shape=tuple(outputs.values()),
        in_specs=[place_of(n) for n in inputs],
        out_specs=tuple(place_of(n) for n in outputs),
        scratch_shapes=list(scratch.values()),
        compiler_params=pltpu.CompilerParams(
            collective_id=collective_id, has_side_effects=True, vmem_limit_bytes=62 * MIB
        ),
    )(*inputs.values())
    return types.SimpleNamespace(**dict(zip(outputs, outs)))


def dma(n):
    return pltpu.SemaphoreType.DMA((n,))


def row_blocks(seq_len, size=256):
    return [slice(i, i + size) for i in range(0, seq_len, size)]


def mixer_constants(k, own, y, c):
    seq_len = k.segc_v.shape[0]
    pack = k.deal[2 * own + y]
    ends = [k.lengths[0, pack]]
    for i in (1, 2):
        ends.append(ends[-1] + k.lengths[i, pack])
    for ref, dims, axis in ((k.segc_v, (seq_len, 128), 0), (k.segr_v, (8, seq_len), 1)):
        place_of = lax.broadcasted_iota(jnp.int32, dims, axis)
        ref[...] = sum((place_of >= end).astype(jnp.int32) for end in ends)
    heads = k.heads[...]
    heads = jnp.where(c == 0, heads, pltpu.roll(heads, 128 - CHIP_HEADS, 1))
    heads = jnp.where(lanes(8) < CHIP_HEADS, heads, 0.0)
    k.par_v[0:1, :] = heads[0:1, :]
    k.par_v[1:2, :] = jnp.where(lanes(1) < CHIP_HEADS, -jnp.exp(heads[1:2, :]), 0.0)
    k.wide_v[...] = dot(jnp.broadcast_to(heads[2:3, :], (8, 128)), k.spread_v[...].astype(F32), precision=lax.Precision.HIGHEST)


def forward_fused(k):
    z, x, y, c = place()
    own = 2 * z + x
    partner = device(z, x, y, 1 - c)
    mover = Mover(k.local)
    lane = lambda start, size: pl.ds(pl.multiple_of(start, 128), size)
    half = k.dn.shape[0] // 2
    for side in range(2):
        for d in range(8):
            mover.load(k.gu.at[:, lane(side * FF + (2 * d + c) * half, half)], k.gu_s.at[:, side * FF // 2 + d * half : side * FF // 2 + (d + 1) * half])
    shard_loads, mover.loads = mover.loads, {}
    for src, dst in ((k.rows, k.rows_v), (k.w_in, k.w_in_v), (k.spread, k.spread_v), (k.cosine, k.cosine_v), (k.sine, k.sine_v)):
        mover.load(src, dst)
    greet(chip_peers())
    columns = lane(k.part_v.shape[1] // 2 * c, k.part_v.shape[1] // 2)
    pairs = (
        (k.ssm.at[:, columns], k.ssm_all),
        (k.att.at[:, columns], k.att_all),
        (k.gu_s, k.gu_w),
        (k.dn.at[pl.ds(half * c, half)], k.dn_w),
    )
    gathers = [Gather(a, b, (k.gsend, k.grecv), ARRAY_SENDS * i, k.own.at[i]) for i, (a, b) in enumerate(pairs)]
    cots = Cotangents(k.cot, k.cots_v, (k.csend, k.crecv), k.own.at[4])
    halves = [Halves(g, out, (k.csend, k.crecv), 3 + i, k.own.at[5 + i]) for i, (g, out) in enumerate(zip(gathers, (k.ssm_v, k.att_v)))]
    gathers[0].start()
    gathers[1].start()
    cots.start()
    for copies in shard_loads.values():
        for copy in copies:
            copy.wait()
    steps = gather_steps(gathers)
    at = steps.index(1) + 6
    steps[at:at] = [h.start for h in halves] + [9]
    steps.insert(steps.index(3) - 2, cots.forward)
    tick = Ticker(steps, 60)

    blocks = row_blocks(k.rows_v.shape[0])
    mover.need(k.rows_v, k.w_in_v)
    tile = k.w_in_v[:, T0 : T0 + 128].astype(F32).T
    k.gains_v[0:1, :] = tile[CHIP_HEADS : CHIP_HEADS + 1, :]
    k.gains_v[1:2, :] = tile[CHIP_HEADS + 1 : CHIP_HEADS + 2, :]
    mover.store(k.gains_v, k.gains)
    for rows in blocks:
        xs = k.rows_v[rows, :].astype(F32)
        unit, _ = rms_parts(xs)
        normed = (unit * k.gains_v[0:1, :]).astype(BF)
        k.normed_v[rows, :] = normed
        for n in range(0, COLS, 768):
            k.proj_v[rows, n : n + 768] = dot(normed, k.w_in_v[:, n : n + 768]).astype(BF)
            tick()
    mover.store(k.proj_v, k.proj)
    kept_normed = mover.store(k.normed_v, k.normed)
    mover.need(k.spread_v, k.cosine_v, k.sine_v)
    mixer_constants(k, own, y, c)
    for src, dst in ((k.segc_v, k.segc), (k.segr_v, k.segr), (k.par_v, k.par), (k.wide_v, k.wide)):
        mover.store(src, dst)
    attention_forward(k.proj_v, k.cosine_v, k.sine_v, k.segc_v, k.segr_v, k.attn_v, k.lse_v, tick)
    mover.store(k.attn_v, k.attn)
    mover.store(k.lse_v, k.lse)
    scan_forward(k.proj_v, k.segc_v, k.segr_v, k.par_v, k.spread_v, k.wide_v, k.gated_v, k.y_v, k.states_v, k.state, tick)
    mover.store(k.gated_v, k.gated)
    mover.store(k.y_v, k.y)
    mover.store(k.states_v, k.states)

    tick.reach(9)
    for h in halves:
        h.arrive()
    mover.store(k.ssm_v, k.w_ssm)
    mover.store(k.att_v, k.w_att)
    sent = []
    for i, rows in enumerate(blocks):
        part = dot(k.gated_v[rows, :], k.ssm_v[...].reshape(XW, -1))
        part = part + dot(k.attn_v[rows, :], k.att_v[...].reshape(QW, -1))
        k.part_v[rows, :] = part.astype(BF)
        sent.append(send(k.part_v.at[rows], k.got_v.at[rows], (k.psend, k.precv), i, partner))
        tick()
    kept_normed.wait()
    mover.stores = [v for v in mover.stores if v is not kept_normed]
    for i, rows in enumerate(blocks):
        landed(k.got_v.at[rows], (k.psend, k.precv), i, partner)
        middle = k.rows_v[rows, :].astype(F32) + (k.part_v[rows, :].astype(F32) + k.got_v[rows, :].astype(F32))
        k.middle_v[rows, :] = middle
        unit, _ = rms_parts(middle)
        k.normed_v[rows, :] = (unit * k.gains_v[1:2, :]).astype(BF)
        tick()
    mover.store(k.middle_v, k.middle)
    mover.store(k.normed_v, k.h2)

    tick.reach(2)
    gathers[2].arrive()
    mover.store(k.gu_w, k.w_gu)
    for rows in blocks:
        for n in range(0, FF // 2, 512):
            for side in (0, FF // 2):
                cols = slice(side + n, side + n + 512)
                w = k.gu_w[:, :, cols].reshape(-1, 512)
                k.w_in_v[rows, cols] = dot(k.normed_v[rows, :], w).astype(BF)
            gate = k.w_in_v[rows, n : n + 512].astype(F32)
            up = k.w_in_v[rows, FF // 2 + n : FF // 2 + n + 512].astype(F32)
            k.act_v[rows, n : n + 512] = (silu(gate) * up).astype(BF)
            tick()
    mover.store(k.w_in_v.at[:, 0:FF], k.hidden)
    mover.store(k.act_v, k.act)
    tick.drain()
    cots.arrive()
    mover.store(k.cots_v, k.cots)
    width = k.rows_v.shape[1]
    for m in range(0, FF // 2, 256):
        k.gdn_v[m : m + 256, :] = dot(k.act_v[:, m : m + 256], k.cots_v[...].reshape(-1, width), ((0,), (0,))).astype(BF)
    mover.store(k.gdn_v, k.g_dn)
    gathers[3].arrive()
    mover.store(k.dn_w, k.w_dn)
    for g in gathers:
        g.finish()
    cots.finish()
    for copy in sent:
        copy.wait_send()
    mover.flush()


def forward_stage(rows, w_in, tables, heads, deal, lengths, cot, shards):
    seq_len, width = rows.shape
    ssm, att, gu, dn = shards
    cosine, sine, spread = tables
    chunks = seq_len // CHUNK
    total = 4 * ARRAY_SENDS
    half = dn.shape[0] // 2
    inputs = dict(
        rows=rows, w_in=w_in, cosine=cosine, sine=sine, spread=spread, heads=heads, deal=deal, lengths=lengths, cot=cot, ssm=ssm, att=att, gu=gu, dn=dn
    )
    spaces = dict(heads=VM, deal=pltpu.SMEM, lengths=pltpu.SMEM)
    square = shape((seq_len, width))
    outputs = dict(
        proj=shape((seq_len, COLS)),
        normed=square,
        gains=shape((8, width), F32),
        attn=shape((seq_len, QW)),
        lse=shape((seq_len, 128), F32),
        gated=shape((seq_len, XW)),
        y=shape((seq_len, XW), F32),
        states=shape((chunks, NS, XW), F32),
        w_ssm=shape((4, ssm.shape[0], width)),
        w_att=shape((4, att.shape[0], width)),
        w_gu=shape((8, gu.shape[0], FF)),
        w_dn=shape((8, half, width)),
        middle=shape((seq_len, width), F32),
        h2=square,
        hidden=shape((seq_len, FF)),
        act=shape((seq_len, FF // 2)),
        cots=shape((4,) + cot.shape[1:]),
        g_dn=shape((FF // 2, width)),
        segc=shape((seq_len, 128), jnp.int32),
        segr=shape((8, seq_len), jnp.int32),
        par=shape((8, 128), F32),
        wide=shape((8, XW), F32),
    )
    out = types.SimpleNamespace(**outputs)
    buffer = lambda v: VM(v.shape, v.dtype)
    scratch = dict(
        rows_v=buffer(rows),
        w_in_v=buffer(w_in),
        cosine_v=buffer(cosine),
        sine_v=buffer(sine),
        spread_v=buffer(spread),
        segc_v=buffer(out.segc),
        segr_v=buffer(out.segr),
        par_v=buffer(out.par),
        wide_v=buffer(out.wide),
        proj_v=buffer(out.proj),
        normed_v=buffer(square),
        gains_v=buffer(out.gains),
        attn_v=buffer(out.attn),
        lse_v=buffer(out.lse),
        gated_v=buffer(out.gated),
        y_v=buffer(out.y),
        states_v=buffer(out.states),
        middle_v=buffer(out.middle),
        act_v=buffer(out.act),
        cots_v=buffer(out.cots),
        ssm_v=buffer(out.w_ssm),
        att_v=buffer(out.w_att),
        gu_w=buffer(out.w_gu),
        dn_w=buffer(out.w_dn),
        gu_s=VM((gu.shape[0], FF), BF),
        ssm_all=VM((8, ssm.shape[0], width // 2), BF),
        att_all=VM((8, att.shape[0], width // 2), BF),
        gdn_v=buffer(out.g_dn),
        part_v=buffer(square),
        got_v=buffer(square),
        state=VM((NS, XW), F32),
        gsend=dma(total),
        grecv=dma(total),
        csend=dma(5),
        crecv=dma(5),
        psend=dma(4),
        precv=dma(4),
        own=dma(7),
        local=dma(48),
    )
    return fused_call(forward_fused, "forward", inputs, outputs, scratch, spaces, 1)


def feed_forward_fused(k):
    z, x, y, c = place()
    partner = device(z, x, y, 1 - c)
    ypeer = device(z, x, 1 - y, c)
    mover = Mover(k.local)
    for src, dst in k.loads:
        mover.load(src, dst)
    greet(chip_peers())
    pairs = ((k.g_dn_v, k.red_dn), (k.gate_v, k.red_gate))
    sums = [Reduce(part, out, *k.bufs[4 * i : 4 * i + 4], (k.rsend, k.rrecv), REDUCE_SENDS * i) for i, (part, out) in enumerate(pairs)]
    mover.need(k.g_dn_v)
    sums[0].start()
    tick = Ticker(reduce_steps(sums, partner))
    seq_len, width = k.middle_v.shape
    span = seq_len // 4
    blocks = row_blocks(seq_len)
    half = FF // 2
    flat = lambda ref: ref[...].reshape(-1, ref.shape[-1])
    pair = (k.psend, k.precv)

    mover.need(k.cots_v, k.w_dn_v, k.hidden_v)
    for i, rows in enumerate(blocks):
        g_act = dot(k.cots_v[i], flat(k.w_dn_v), ((1,), (1,))).astype(BF).astype(F32)
        gate = k.hidden_v[rows, :half].astype(F32)
        up = k.hidden_v[rows, half:].astype(F32)
        sig = 1.0 / (1.0 + jnp.exp(-gate))
        k.hidden_v[rows, :half] = (g_act * up * (sig * (1.0 + gate * (1.0 - sig)))).astype(BF)
        k.hidden_v[rows, half:] = (g_act * (gate * sig)).astype(BF)
    mover.need(k.h2_v)
    tick.plan(2, 4)
    for d in range(0, 8, 2):
        grad = dot(k.h2_v[:, 128 * d : 128 * d + 256], k.hidden_v[:, :half], ((0,), (0,))).astype(BF)
        k.gate_v[d : d + 2] = grad.reshape(2, 128, half)
        tick()
    sums[1].start()
    tick.plan(13, 24)
    mover.need(k.w_gu_v)
    sent = []
    for i, rows in enumerate(blocks):
        part = dot(k.hidden_v[rows, :], flat(k.w_gu_v), ((1,), (1,)))
        k.part_v[rows, :] = part.astype(BF)
        sent.append(send(k.part_v.at[rows], k.got_v.at[rows], pair, i, partner))
        tick()
    mover.need(k.act_v)
    for j in range(2):
        rows = pl.ds(pl.multiple_of((2 * j + 1 - c) * span, span), span)
        k.opart_v[j] = dot(k.act_v[rows, :], flat(k.w_dn_v)).astype(BF)
        sent.append(send(k.opart_v.at[j], k.ogot_v.at[j], pair, 4 + j, partner))
        tick()
    for d in range(0, 8, 2):
        grad = dot(k.h2_v[:, 128 * d : 128 * d + 256], k.hidden_v[:, half:], ((0,), (0,))).astype(BF)
        k.up_v[d : d + 2] = grad.reshape(2, 128, half)
        tick()
    mover.store(k.up_v, k.g_up)

    mover.need(k.middle_v)
    for j in range(2):
        rows = pl.ds(pl.multiple_of((2 * j + c) * span, span), span)
        own = k.middle_v[rows, :] + dot(k.act_v[rows, :], flat(k.w_dn_v)).astype(BF).astype(F32)
        landed(k.ogot_v.at[j], pair, 4 + j, partner)
        k.out_v[j] = (own + k.ogot_v[j].astype(F32)).astype(BF)
        tick()
    sent.append(send(k.out_v.at[1 - y], k.output.at[y], pair, 14, ypeer))
    mover.store(k.out_v.at[y], k.output.at[y])

    mover.need(k.middle_v, k.gains_v, k.w_ssm_v, k.w_att_v)
    gain = k.gains_v[1:2, :]
    grad_gain = jnp.zeros((1, width), F32)
    for i, rows in enumerate(blocks):
        landed(k.got_v.at[rows], pair, i, partner)
        g_two = (k.part_v[rows, :].astype(F32) + k.got_v[rows, :].astype(F32)).astype(BF).astype(F32)
        unit, scale = rms_parts(k.middle_v[rows, :])
        grad_gain = grad_gain + jnp.sum(g_two * unit, axis=0, keepdims=True)
        g_mid = k.cots_v[i].astype(F32) + rms_back(unit, scale, gain, g_two)
        k.got_f32[rows, :] = g_mid
        branch = g_mid.astype(BF)
        k.branch_v[rows, :] = branch
        tick()
        k.ggated_v[rows, :] = dot(branch, flat(k.w_ssm_v), ((1,), (1,))).astype(BF)
        k.gattn_v[rows, :] = dot(branch, flat(k.w_att_v), ((1,), (1,))).astype(BF)
        tick()
    k.gffn_v[0:1, :] = 0.5 * grad_gain
    mover.store(k.gffn_v, k.gffn)
    mover.store(k.ggated_v, k.ggated)
    mover.store(k.gattn_v, k.gattn)
    for j in range(2):
        mover.store(k.got_f32.at[pl.ds(pl.multiple_of((2 * j + c) * span, span), span)], k.g_mid.at[j])

    mover.need(k.gated_v, k.attn_v)
    moves = []
    n = 6
    for source, rows, hold, out in ((k.gated_v, XW, k.gssm_v, k.g_ssm), (k.attn_v, QW, k.gatt_v, k.g_att)):
        for m in range(0, rows, 256):
            hold[m : m + 256, :] = dot(source[:, m : m + 256], k.branch_v[...], ((0,), (0,))).astype(BF)
            tick()
        own = rows // 4
        for d in range(4):
            columns = lambda e: hold.at[pl.ds(d * own, own), pl.ds(pl.multiple_of(e * (width // 2), 128), width // 2)]
            mover.store(columns(c), out.at[4 * c + d])
            moves.append((out.at[4 * (1 - c) + d], n))
            sent.append(send(columns(1 - c), out.at[4 * c + d], pair, n, partner))
            n += 1

    tick.drain()
    for s in sums:
        s.finish(partner)
    for ref, i in moves:
        landed(ref, pair, i, partner)
    landed(k.output.at[1 - y], pair, 14, ypeer)
    for copy in sent:
        copy.wait_send()
    mover.flush()


def reduce_scratch(shapes):
    bufs = []
    for dims in shapes:
        half = (dims[1] // 2, dims[2])
        bufs += [VM((4,) + half, BF)] * 3 + [VM((3,) + half, BF)]
    return {"b" + str(i): b for i, b in enumerate(bufs)}


def loaded(inputs, names=None):
    return {n + "_v": VM(v.shape, v.dtype) for n, v in inputs.items()}


def with_lists(kernel, inputs, bufs):
    def run(k):
        refs = vars(k)
        k.loads = [(refs[n], refs[n + "_v"]) for n in inputs if n + "_v" in refs]
        k.bufs = [refs[n] for n in bufs]
        kernel(k)

    return run


def feed_forward_stage(f):
    seq_len, width = f.middle.shape
    inputs = dict(
        g_dn=f.g_dn.reshape(8, -1, width),
        cots=f.cots,
        w_dn=f.w_dn,
        hidden=f.hidden,
        h2=f.h2,
        w_gu=f.w_gu,
        act=f.act,
        middle=f.middle,
        gains=f.gains,
        w_ssm=f.w_ssm,
        w_att=f.w_att,
        gated=f.gated,
        attn=f.attn,
    )
    span = seq_len // 4
    part = (8, width // 8, FF // 2)
    outputs = dict(
        output=shape((2, span, width)),
        red_dn=shape((2,) + inputs["g_dn"].shape[1:]),
        red_gate=shape((2,) + part[1:]),
        g_up=shape(part),
        g_ssm=shape((8, XW // 4, width // 2)),
        g_att=shape((8, QW // 4, width // 2)),
        ggated=shape((seq_len, XW)),
        gattn=shape((seq_len, QW)),
        g_mid=shape((2, span, width), F32),
        gffn=shape((8, width), F32),
    )
    bufs = reduce_scratch([inputs["g_dn"].shape, part])
    scratch = dict(
        **loaded(inputs),
        **bufs,
        gate_v=VM(part, BF),
        up_v=VM(part, BF),
        part_v=VM((seq_len, width), BF),
        got_v=VM((seq_len, width), BF),
        opart_v=VM((2, span, width), BF),
        ogot_v=VM((2, span, width), BF),
        out_v=VM((2, span, width), BF),
        got_f32=VM((seq_len, width), F32),
        branch_v=VM((seq_len, width), BF),
        ggated_v=VM((seq_len, XW), BF),
        gattn_v=VM((seq_len, QW), BF),
        gssm_v=VM((XW, width), BF),
        gatt_v=VM((QW, width), BF),
        gffn_v=VM((8, width), F32),
        rsend=dma(2 * REDUCE_SENDS),
        rrecv=dma(2 * REDUCE_SENDS),
        psend=dma(15),
        precv=dma(15),
        local=dma(32),
    )
    kernel = with_lists(feed_forward_fused, inputs, bufs)
    return fused_call(kernel, "feed_forward", inputs, outputs, scratch, dict(red_dn=VM, red_gate=VM), 2)


def backward_fused(k):
    z, x, y, c = place()
    own = 2 * z + x
    slot = 2 * own + y
    partner = device(z, x, y, 1 - c)
    others = [(r, i, j) for r in range(4) for i in range(2) for j in range(2) if r or i or j]
    targets = [device(z ^ r, x ^ i, y ^ j, c) for r, i, j in others]
    mover = Mover(k.local)
    for src, dst in k.loads:
        mover.load(src, dst)
    greet(targets + [partner])
    pairs = (
        (k.up_v, k.red_up),
        (k.ssm_v, k.red_ssm),
        (k.att_v, k.red_att),
        (k.gz_v, k.red_gz),
        (k.xbc_v, k.red_xbc),
        (k.qkv_v, k.red_qkv),
        (k.steps_v, k.red_steps),
    )
    sums = [Reduce(part, out, *k.bufs[4 * i : 4 * i + 4], (k.rsend, k.rrecv), REDUCE_SENDS * i) for i, (part, out) in enumerate(pairs)]
    mover.need(k.up_v)
    sums[0].start()
    mover.need(k.ssm_v, k.att_v)
    for step in sums[1:3]:
        step.start()
    tick = Ticker(reduce_steps(sums, partner))
    tick.plan(2, 8)
    seq_len, width = k.normed_v.shape
    span = seq_len // 4

    def grad_of(lo, hi, out, at):
        for d in range(0, 8, 2):
            grad = dot(k.normed_v[:, 128 * d : 128 * d + 256], k.gproj_v[:, lo:hi], ((0,), (0,))).astype(BF)
            out[d : d + 2, :, at : at + hi - lo] = grad.reshape(2, 128, hi - lo)
            tick()

    mover.need(k.proj_v, k.segc_v, k.segr_v, k.par_v, k.spread_v, k.wide_v, k.ggated_v, k.y_v)
    gate_backward(k.proj_v, k.wide_v, k.y_v, k.ggated_v, k.gproj_v, k.ggated_v, tick)
    mover.need(k.normed_v)
    grad_of(Z0, Z0 + XW, k.gz_v, 0)
    sums[3].start()
    mover.need(k.states_v)
    tick.plan(14, 24)
    scan_backward(k.proj_v, k.segc_v, k.segr_v, k.par_v, k.spread_v, k.wide_v, k.y_v, k.states_v, k.ggated_v, k.gproj_v, k.gpar_v, k.gstate, tick)
    grad_of(X0, X0 + XW, k.xbc_v, 0)
    grad_of(B0, T0, k.xbc_v, XW)
    sums[4].start()
    tick.plan(13, 20)
    mover.need(k.gattn_v, k.attn_v, k.lse_v, k.cosine_v, k.sine_v)
    attention_backward(k.proj_v, k.cosine_v, k.sine_v, k.segc_v, k.segr_v, k.attn_v, k.lse_v, k.gattn_v, k.gproj_v, k.gkv, tick)
    grad_of(Q0, B0, k.qkv_v, 0)
    sums[5].start()
    tick.plan(6, 4)
    pair = (k.psend, k.precv)
    mover.need(k.w_in_v, k.rows_v, k.g_mid_v, k.gains_v, k.gffn_v)
    sent = []
    for j in range(2):
        rows = pl.ds(pl.multiple_of((2 * j + 1 - c) * span, span), span)
        k.opart_v[j] = dot(k.gproj_v[rows, :], k.w_in_v[...], ((1,), (1,))).astype(BF)
        sent.append(send(k.opart_v.at[j], k.ogot_v.at[j], pair, j, partner))
        tick()
    gain = k.gains_v[0:1, :]
    grad_gain = jnp.zeros((1, width), F32)
    columns = lambda d: pl.ds(pl.multiple_of(d * 128, 128), 128)
    sems = (k.dsend, k.drecv)
    for j in range(2):
        rows = pl.ds(pl.multiple_of((2 * j + c) * span, span), span)
        part = dot(k.gproj_v[rows, :], k.w_in_v[...], ((1,), (1,))).astype(BF).astype(F32)
        landed(k.ogot_v.at[j], pair, j, partner)
        g_h1 = (part + k.ogot_v[j].astype(F32)).astype(BF).astype(F32)
        unit, scale = rms_parts(k.rows_v[rows, :].astype(F32))
        grad_gain = grad_gain + jnp.sum(g_h1 * unit, axis=0, keepdims=True)
        k.ogot_v[j] = (k.g_mid_v[j] + rms_back(unit, scale, gain, g_h1)).astype(BF)
        tick()
    mover.store(k.ogot_v.at[y, :, columns(own)], k.returned.at[slot])
    for i, (r, a, b) in enumerate(others):
        d = 2 * (z ^ r) + (x ^ a)
        sent.append(send(k.ogot_v.at[y ^ b, :, columns(d)], k.returned.at[slot], sems, i, targets[i]))
    valid = lanes(1) < CHIP_HEADS
    heads = [jnp.where(valid, k.gpar_v[p : p + 1, :], 0.0) for p in range(3)]
    lines = [grad_gain, k.gffn_v[0:1, :]] + [jnp.concatenate([h] * (width // 128), axis=1) for h in heads]
    extra = jnp.concatenate([jnp.zeros((CHIP_HEADS, width), F32)] + lines + [jnp.zeros((STEP_ROWS - CHIP_HEADS - 5, width), F32)], axis=0)
    grad = dot(k.gproj_v[:, T0:COLS], k.normed_v[...], ((0,), (0,)))[0:STEP_ROWS, :] + extra
    for d in range(8):
        k.steps_v[d] = grad[:, 128 * d : 128 * (d + 1)].astype(BF)
    sums[6].start()
    tick.drain()
    for s in sums:
        s.finish(partner)
    for i, (r, a, b) in enumerate(others):
        landed(k.returned.at[2 * (2 * (z ^ r) + (x ^ a)) + (y ^ b)], sems, i, targets[i])
    for copy in sent:
        copy.wait_send()
    mover.flush()


STEP_ROWS = 32


def backward_stage(f, m, rows, w_in, tables):
    seq_len, width = rows.shape
    span = seq_len // 4
    cosine, sine, spread = tables
    inputs = dict(
        up=m.g_up,
        ssm=m.g_ssm,
        att=m.g_att,
        proj=f.proj,
        segc=f.segc,
        segr=f.segr,
        par=f.par,
        spread=spread,
        wide=f.wide,
        ggated=m.ggated,
        y=f.y,
        normed=f.normed,
        states=f.states,
        gattn=m.gattn,
        attn=f.attn,
        lse=f.lse,
        cosine=cosine,
        sine=sine,
        w_in=w_in,
        rows=rows,
        g_mid=m.g_mid,
        gains=f.gains,
        gffn=m.gffn,
    )
    block = width // 8
    new = dict(
        gz_v=(8, block, XW), xbc_v=(8, block, XW + 256), qkv_v=(8, block, QW + 128), steps_v=(8, STEP_ROWS, block)
    )
    parts = [m.g_up.shape, m.g_ssm.shape, m.g_att.shape] + list(new.values())
    out = [shape((2,) + d[1:]) for d in parts]
    outputs = dict(
        red_up=out[0],
        red_ssm=out[1],
        red_att=out[2],
        red_gz=out[3],
        red_xbc=out[4],
        red_qkv=out[5],
        red_steps=out[6],
    )
    spaces = {n: VM for n in outputs}
    outputs.update(returned=shape((16, span, 128)))
    bufs = reduce_scratch(parts)
    scratch = dict(
        **loaded(inputs),
        **bufs,
        **{n: VM(d, BF) for n, d in new.items()},
        gproj_v=VM((seq_len, COLS), BF),
        gpar_v=VM((8, 128), F32),
        gkv=VM((seq_len, 256), F32),
        gstate=VM((NS, XW), F32),
        opart_v=VM((2, span, width), BF),
        ogot_v=VM((2, span, width), BF),
        rsend=dma(len(parts) * REDUCE_SENDS),
        rrecv=dma(len(parts) * REDUCE_SENDS),
        psend=dma(2),
        precv=dma(2),
        dsend=dma(15),
        drecv=dma(15),
        local=dma(28),
    )
    return fused_call(with_lists(backward_fused, inputs, bufs), "mixer_backward", inputs, outputs, scratch, spaces, 3)


def finish_kernel(deal, *refs):
    sources, (tokens, g_in, g_dt, g_ssm, g_att, g_gu, g_dn, small), refs = refs[:10], refs[10:18], refs[18:]
    held, (sems, load_sems) = refs[:10], refs[10:]
    up, gate, dn, ssm, att, gz, xbc, qkv, steps, returned = held
    loads = [pltpu.make_async_copy(src, dst, load_sems.at[i]) for i, (src, dst) in enumerate(zip(sources, held))]
    for copy in reversed(loads):
        copy.start()
    for copy in reversed(loads):
        copy.wait()
    copies = [pltpu.make_async_copy(returned.at[j], tokens.at[deal[j]], sems.at[j]) for j in range(16)]
    for copy in copies:
        copy.start()
    wide = lambda v: v.astype(F32)
    inner = MH * HP
    q_start = 2 * inner + 2 * NS
    kv_start = q_start + QUERY_HEADS * HEAD_WIDTH
    half = dn.shape[1]
    for c in range(2):
        g_in[:, XW * c : XW * (c + 1)] = wide(gz[c])
        g_in[:, inner + XW * c : inner + XW * (c + 1)] = wide(xbc[c, :, 0:XW])
        g_in[:, q_start + QW * c : q_start + QW * (c + 1)] = wide(qkv[c, :, 0:QW])
        g_ssm[:, ssm.shape[2] * c : ssm.shape[2] * (c + 1)] = wide(ssm[c])
        g_att[:, att.shape[2] * c : att.shape[2] * (c + 1)] = wide(att[c])
        g_dn[half * c : half * (c + 1), :] = wide(dn[c])
        for d in range(8):
            at = (2 * d + c) * half
            g_gu[:, at : at + half] = wide(gate[c, :, half * d : half * (d + 1)])
            g_gu[:, FF + at : FF + at + half] = wide(up[c, :, half * d : half * (d + 1)])
    g_in[:, 2 * inner : q_start] = wide(xbc[0, :, XW:]) + wide(xbc[1, :, XW:])
    kv = [wide(qkv[c, :, QW : QW + 128]) for c in range(2)]
    low_lanes = lanes(kv[0].shape[0]) < 64
    g_in[:, kv_start : kv_start + 128] = jnp.where(low_lanes, kv[0], pltpu.roll(kv[1], 64, 1))
    g_in[:, kv_start + 128 : kv_start + 256] = jnp.where(low_lanes, pltpu.roll(kv[0], 64, 1), kv[1])
    first, second = wide(steps[0]), wide(steps[1])
    line = lax.broadcasted_iota(jnp.int32, first.shape, 0)
    heads = jnp.where(line < CHIP_HEADS, first, pltpu.roll(second, CHIP_HEADS, 0))
    heads = jnp.concatenate([heads, jnp.zeros((128 - STEP_ROWS, 128), F32)], axis=0).T
    g_dt[...] = heads[:, 0:MH]
    small[...] = jnp.zeros_like(small)
    for i in range(2):
        row = CHIP_HEADS + i
        small[i : i + 1, :] = first[row : row + 1, :] + second[row : row + 1, :]
    for i in range(3):
        row = CHIP_HEADS + 2 + i
        moved = pltpu.roll(second[row : row + 1, :], CHIP_HEADS, 1)
        small[2 + i : 3 + i, :] = jnp.where(lanes(1) < CHIP_HEADS, first[row : row + 1, :], moved)
    for copy in copies:
        copy.wait()


def finish_stage(deal, m, b, ssm_out, attn_out, down_proj, in_proj):
    returned = b.returned
    sources = (b.red_up, m.red_gate, m.red_dn, b.red_ssm, b.red_att, b.red_gz, b.red_xbc, b.red_qkv, b.red_steps, returned)
    wide = lambda v: shape(v.shape, F32)
    block = in_proj.shape[0]
    return pl.pallas_call(
        finish_kernel,
        name="place_gradients",
        out_shape=(
            shape(returned.shape),
            wide(in_proj),
            shape((block, MH), F32),
            wide(ssm_out),
            wide(attn_out),
            shape((block, 2 * FF), F32),
            wide(down_proj),
            shape((8, 128), F32),
        ),
        in_specs=[pl.BlockSpec(memory_space=pltpu.SMEM)] + any_specs(10),
        out_specs=tuple(any_specs(1) + whole(7)),
        scratch_shapes=[VM(v.shape, v.dtype) for v in sources] + [dma(16), dma(10)],
        compiler_params=pltpu.CompilerParams(vmem_limit_bytes=62 * MIB),
    )(deal, *sources)


def mixer_tables(seq_len):
    half = HEAD_WIDTH // 2
    frequency = np.float32(THETA) ** (-np.arange(half, dtype=np.float32) * np.float32(2.0 / HEAD_WIDTH))
    angles = np.arange(seq_len, dtype=np.float32)[:, None] * frequency[None, :].astype(np.float32)
    cosine = np.tile(np.cos(angles), (1, 4)).astype(np.float32)
    sine = np.tile(np.concatenate([-np.sin(angles), np.sin(angles)], axis=1), (1, 2)).astype(np.float32)
    head_of = np.arange(XW) // HP
    spread = np.arange(128)[:, None] % 64 == head_of[None, :]
    return jnp.asarray(cosine), jnp.asarray(sine), jnp.asarray(spread, BF)


def fused_layer(dealt, cot, seq_lengths, deal_order, gains, in_proj, dt_proj, head_values, ssm_out, attn_out, gate_up, down_proj):
    block = in_proj.shape[0]
    width = cot.shape[2]
    seq_len = 4 * cot.shape[1]
    beside = jnp.concatenate([dt_proj.T] + [g[None] for g in gains] + [jnp.zeros((128 - MH - 2, block), BF)], axis=0)
    heads = jnp.pad(jnp.stack(head_values), ((0, 5), (0, 128 - MH)))
    tables = mixer_tables(seq_len)
    rows, w_in = start_transfers(dealt, in_proj, beside)
    rows, w_in = rows.reshape(seq_len, width), w_in.reshape(width, COLS)
    first = forward_stage(rows, w_in, tables, heads, deal_order, seq_lengths.T, cot, (ssm_out, attn_out, gate_up, down_proj))
    mid = feed_forward_stage(first)
    last = backward_stage(first, mid, rows, w_in, tables)
    tokens, g_in, g_dt, g_ssm, g_att, g_gu, g_dn, small = finish_stage(deal_order, mid, last, ssm_out, attn_out, down_proj, in_proj)
    heads = [small[2 + i, :MH] for i in range(3)]
    return (mid.output, tokens, small[0], g_in, g_dt, *heads, g_ssm, g_att, small[1], g_gu, g_dn)


def rms_parts(v):
    scale = lax.rsqrt(jnp.mean(v * v, axis=-1, keepdims=True) + EPS)
    return v * scale, scale


def rms_back(normed, scale, gain, grad):
    inner = grad * gain
    return scale * (inner - normed * jnp.mean(inner * normed, axis=-1, keepdims=True))


def silu(v):
    return v / (1.0 + jnp.exp(-v))


def low(v):
    return v.astype(BF)


def plain_start(dealt, cot, w, y):
    arrived = lax.all_to_all(dealt, "dp", split_axis=0, concat_axis=2, tiled=True)
    rows = lax.all_gather(arrived, "seq", axis=1, tiled=True)
    cots = lax.all_gather(cot, "seq", axis=1, tiled=True)
    pick = lambda v: lax.dynamic_index_in_dim(v, y, 0, keepdims=False)
    return pick(rows), lax.all_gather(w, "dp", axis=0, tiled=True), pick(cots)


def plain_gather(ssm, att, gu, dn, c):
    every = [lax.all_gather(v, "dp", axis=0, tiled=True) for v in (ssm, att, gu, dn)]
    out = []
    for v in every[:2]:
        rows = v.shape[0] // 2
        mine = lax.all_gather(v, "seq", axis=1, tiled=True)[:, : 2 * v.shape[1]]
        out.append(lax.dynamic_slice_in_dim(mine, c * rows, rows))
    return out + every[2:]


def plain_pair(part):
    return lax.ppermute(part, "seq", [(0, 1), (1, 0), (2, 3), (3, 2)])


def plain_reduce(parts, out_rows, gx, y, c):
    reduced = []
    for p in parts:
        total = lax.psum_scatter(p.reshape(-1, p.shape[-1]), "dp", scatter_dimension=0, tiled=True)
        every = lax.all_gather(total, "seq", axis=0).astype(F32)
        reduced.append(jnp.stack([every[0] + every[2], every[1] + every[3]]))
    peer = lax.ppermute(out_rows, "seq", [(0, 2), (1, 3), (2, 0), (3, 1)])
    output = jnp.where(jnp.arange(2)[:, None, None] == y, out_rows, jnp.flip(peer, 0))
    whole_rows = lax.all_gather(gx, "seq", axis=0)
    slot = 2 * y + c
    by_pack = lax.dynamic_index_in_dim(whole_rows, c, 0, False), lax.dynamic_index_in_dim(whole_rows, c + 2, 0, False)
    both = jnp.stack([lax.dynamic_index_in_dim(v, y, 0, False) for v in by_pack])
    returned = lax.all_to_all(both, "dp", split_axis=2, concat_axis=0, tiled=True)
    return reduced, output, returned


def plain_layer(dealt, cot, w_in, shards, consts, y, c):
    groups = lax.axis_size("dp")
    rows, w_in, cots = plain_start(dealt, cot, w_in, y)
    w_ssm, w_att, w_gu, w_dn = plain_gather(*shards, c)
    span, width = cot.shape[1:]
    block = width // groups
    cut = lambda v, start, size: lax.dynamic_slice_in_dim(v, start, size, axis=1)

    x = rows.astype(F32)
    gain_in = w_in[:, T0 + CHIP_HEADS].astype(F32)[None, :]
    gain_ffn = w_in[:, T0 + CHIP_HEADS + 1].astype(F32)[None, :]
    unit_in, scale_in = rms_parts(x)
    normed = low(unit_in * gain_in)
    proj = low(dot(normed, w_in))
    gated, *saved = mixer_forward(proj, consts)
    attn = saved[0]
    part = low(dot(gated, w_ssm) + dot(attn, w_att))
    middle = x + (part.astype(F32) + plain_pair(part).astype(F32))
    unit_ffn, scale_ffn = rms_parts(middle)
    normed_two = low(unit_ffn * gain_ffn)
    gu = low(dot(normed_two, w_gu)).astype(F32)
    gate, up = gu[:, : FF // 2], gu[:, FF // 2 :]
    act = low(silu(gate) * up)
    out_part = low(dot(act, w_dn))
    by_core = lambda v: lax.dynamic_index_in_dim(v.reshape(2, 2, span, width), c, 1, keepdims=False)
    out_rows = low(by_core(middle) + (by_core(out_part).astype(F32) + by_core(plain_pair(out_part)).astype(F32)))

    g_act = low(dot(cots, w_dn, ((1,), (1,)))).astype(F32)
    grad_dn = low(dot(act, cots, ((0,), (0,))))
    sig = 1.0 / (1.0 + jnp.exp(-gate))
    g_gu = low(jnp.concatenate([g_act * up * (sig * (1.0 + gate * (1.0 - sig))), g_act * (gate * sig)], axis=1))
    grad_gu = low(dot(normed_two, g_gu, ((0,), (0,))))
    part = low(dot(g_gu, w_gu, ((1,), (1,))))
    g_two = low(part.astype(F32) + plain_pair(part).astype(F32)).astype(F32)
    g_mid = cots.astype(F32) + rms_back(unit_ffn, scale_ffn, gain_ffn, g_two)
    grad_gain_ffn = 0.5 * jnp.sum(g_two * unit_ffn, axis=0)
    g_branch = low(g_mid)
    g_gated = low(dot(g_branch, w_ssm, ((1,), (1,))))
    g_attn = low(dot(g_branch, w_att, ((1,), (1,))))
    grad_ssm = low(dot(gated, g_branch, ((0,), (0,))))
    grad_att = low(dot(attn, g_branch, ((0,), (0,))))
    g_proj, g_par = mixer_backward(proj, consts, saved, g_gated, g_attn)
    grad_in = dot(normed, g_proj, ((0,), (0,)))
    part = low(dot(g_proj, w_in, ((1,), (1,))))
    g_h1 = low(by_core(part).astype(F32) + by_core(plain_pair(part)).astype(F32)).astype(F32)
    scale_rows = by_core(jnp.broadcast_to(scale_in, x.shape))
    g_x = low(by_core(g_mid) + rms_back(by_core(unit_in), scale_rows, gain_in, g_h1))
    grad_gain_in = jnp.sum(g_h1 * by_core(unit_in), axis=(0, 1))
    head_grads = jnp.tile(jnp.pad(g_par[:3, :CHIP_HEADS].T, ((0, block - CHIP_HEADS), (0, 0))), (groups, 1))
    extra = jnp.concatenate([grad_gain_in[:, None], grad_gain_ffn[:, None], head_grads], axis=1)
    grad_in = low(lax.dynamic_update_slice(grad_in, extra, (0, T0 + CHIP_HEADS)))

    by_block = lambda v: v.reshape(groups, -1, v.shape[-1])
    parts = [by_block(grad_in), by_block(grad_dn), by_block(grad_gu)]
    for v in (grad_ssm, grad_att):
        both = jnp.stack([v, plain_pair(v)])
        both = jnp.where(c == 0, both, both[::-1]).reshape(-1, width)
        parts.append(by_block(cut(both, width // 2 * c, width // 2)))
    reduced, output, returned = plain_reduce(parts, out_rows, g_x, y, c)
    return output, returned, reduced


def body(tokens, cot, seq_lengths, deal_order, in_gain, in_proj, dt_proj, dt_bias, a_log, d_skip, ssm_out, attn_out, ffn_gain, gate_up, down_proj):
    groups = lax.axis_size("dp")
    dealt = tokens.at[deal_order].get(mode="promise_in_bounds")
    if groups == 8:
        return fused_layer(
            dealt, cot, seq_lengths, deal_order, (in_gain, ffn_gain), in_proj, dt_proj, (dt_bias, a_log, d_skip), ssm_out, attn_out, gate_up, down_proj
        )
    dp_index, seq_index = lax.axis_index("dp"), lax.axis_index("seq")
    y, c = seq_index // 2, seq_index % 2
    packs, span, width = cot.shape
    seq_len = span * lax.axis_size("seq")
    inner = MH * HP
    block = in_proj.shape[0]

    cut = lambda v, start, size: lax.dynamic_slice_in_dim(v, start, size, axis=1)
    q_start = 2 * inner + 2 * NS
    k_start = q_start + QUERY_HEADS * HEAD_WIDTH
    v_start = k_start + KEY_VALUE_HEADS * HEAD_WIDTH
    w_in = jnp.concatenate(
        [
            cut(in_proj, XW * c, XW),
            cut(in_proj, inner + XW * c, XW),
            cut(in_proj, q_start + QW * c, QW),
            cut(in_proj, k_start + HEAD_WIDTH * c, HEAD_WIDTH),
            cut(in_proj, v_start + HEAD_WIDTH * c, HEAD_WIDTH),
            in_proj[:, 2 * inner : q_start],
            cut(dt_proj, CHIP_HEADS * c, CHIP_HEADS),
            in_gain[:, None],
            ffn_gain[:, None],
            jnp.zeros((block, 128 - CHIP_HEADS - 2), BF),
        ],
        axis=1,
    )
    half_units = down_proj.shape[0] // 2
    w_gu = gate_up.reshape(block, 2, groups, 2, half_units)
    w_gu = lax.dynamic_index_in_dim(w_gu, c, 3, keepdims=False).reshape(block, FF)
    w_dn = lax.dynamic_slice_in_dim(down_proj, half_units * c, half_units, axis=0)
    w_ssm = cut(ssm_out, width // 2 * c, width // 2)
    w_att = cut(attn_out, width // 2 * c, width // 2)

    pack = lax.dynamic_index_in_dim(deal_order, dp_index * packs + y, 0, keepdims=False)
    ends = jnp.cumsum(lax.dynamic_index_in_dim(seq_lengths, pack, 0, keepdims=False))[:-1]
    places = jnp.arange(seq_len, dtype=jnp.int32)
    seg = jnp.sum((places[:, None] >= ends[None, :]).astype(jnp.int32), axis=1)
    segc = jnp.broadcast_to(seg[:, None], (seq_len, 128))
    segr = jnp.broadcast_to(seg[None, :], (8, seq_len))
    half = HEAD_WIDTH // 2
    frequency = THETA ** (-jnp.arange(half, dtype=F32) * 2.0 / HEAD_WIDTH)
    angles = places.astype(F32)[:, None] * frequency[None, :]
    cosine = jnp.tile(jnp.cos(angles), (1, 4))
    sine = jnp.tile(jnp.concatenate([-jnp.sin(angles), jnp.sin(angles)], axis=1), (1, 2))
    own_heads = lambda v: lax.dynamic_slice_in_dim(v, CHIP_HEADS * c, CHIP_HEADS)
    par = jnp.zeros((8, 128), F32)
    par = par.at[0, :CHIP_HEADS].set(own_heads(dt_bias)).at[1, :CHIP_HEADS].set(-jnp.exp(own_heads(a_log)))
    wide = jnp.broadcast_to(jnp.repeat(own_heads(d_skip), HP)[None, :], (8, XW))
    head_of = jnp.arange(XW) // HP
    spread = (jnp.arange(128)[:, None] % 64 == head_of[None, :]).astype(BF)
    consts = (cosine, sine, segc, segr, par, spread, wide)

    shards = (w_ssm, w_att, w_gu, w_dn)
    output, returned, (r_in, r_dn, r_gu, r_ssm, r_att) = plain_layer(dealt, cot, w_in, shards, consts, y, c)

    both = lambda start, size: [r_in[0, :, start : start + size], r_in[1, :, start : start + size]]
    grad_in_proj = jnp.concatenate(
        both(Z0, XW)
        + both(X0, XW)
        + [r_in[0, :, B0:T0] + r_in[1, :, B0:T0]]
        + both(Q0, QW)
        + both(KV0, HEAD_WIDTH)
        + both(KV0 + HEAD_WIDTH, HEAD_WIDTH),
        axis=1,
    )
    grad_dt_proj = jnp.concatenate(both(T0, CHIP_HEADS), axis=1)
    tail = r_in[:, :, T0 + CHIP_HEADS : T0 + CHIP_HEADS + 5]
    gains = tail[0, :, :2] + tail[1, :, :2]
    heads = tail[:, :CHIP_HEADS, 2:5].reshape(MH, 3)
    grad_gate_up = jnp.stack(
        [r_gu[k].reshape(block, 2, groups, half_units) for k in range(2)], axis=3
    ).reshape(block, 2 * FF)
    side = lambda v: jnp.concatenate([v[0], v[1]], axis=1)
    return (
        output,
        jnp.take(returned, jnp.argsort(deal_order), axis=0),
        gains[:, 0],
        grad_in_proj,
        grad_dt_proj,
        heads[:, 0],
        heads[:, 1],
        heads[:, 2],
        side(r_ssm),
        side(r_att),
        gains[:, 1],
        grad_gate_up,
        r_dn.reshape(-1, width),
    )


def solution(mesh):
    return jax.shard_map(
        body,
        mesh=mesh,
        in_specs=(
            P(None, "seq", "dp"),
            P("dp", "seq", None),
            P(),
            P(),
            P("dp"),
            P("dp", None),
            P("dp", None),
            P(),
            P(),
            P(),
            P("dp", None),
            P("dp", None),
            P("dp"),
            P("dp", None),
            P("dp", None),
        ),
        out_specs=(
            P("dp", "seq", None),
            P(None, "seq", "dp"),
            P("dp"),
            P("dp", None),
            P("dp", None),
            P(),
            P(),
            P(),
            P("dp", None),
            P("dp", None),
            P("dp"),
            P("dp", None),
            P("dp", None),
        ),
        check_vma=False,
    )
```

profile of v0, /device:TPU:9, one launch (start us, length us, event | category | flops | bytes accessed | tf_op | source)
XLA Modules:
  0.0 349.2 jit_solution(7749687645007100305)
XLA Ops:
  0.6 0.0 copy-start
  0.7 0.7 compare_select_fusion
  1.4 0.1 pad.11.clone
  1.5 1.3 select_maximum_fusion.refs_5_
  2.8 1.4 maximum_maximum_fusion.beside
  4.2 0.0 copy-done
  4.2 1.6 gather_fusion
  5.9 59.2 %deal_and_gather.1 = (bf16[4,256,1024]{2,1,0:T(8,128)(2,1)}, bf16[8,128,2304]{2,1,0:T(8,128)(2,1)}) custom-call(bf16[16,256,128]{2,1,0:T(8,128)(2,1)} %gather_fusion, bf16[128,4096]{1,0:T(8,128)(2,1)} %in_proj.1, bf16[128,128]{1,0:T(8,128)(2,1)} %maximum_maximum_fusion.beside), custom_call_target="tpu_custom_call" | custom-call | tf_op jit(solution)/shard_map/deal_and_gather/pallas_call | solution.py:578
  65.1 85.1 %forward.1 = (bf16[1024,2304]{1,0:T(8,128)(2,1)}, bf16[1024,1024]{1,0:T(8,128)(2,1)}, f32[8,1024]{1,0:T(8,128)}, bf16[1024,256]{1,0:T(8,128)(2,1)}, f32[1024,128...) custom-call(bf16[1024,1024]{1,0:T(8,128)(2,1)} %bitcast.22, ...), custom_call_target="tpu_custom_call" | custom-call | tf_op jit(solution)/shard_map/forward/pallas_call | solution.py:844
  150.2 66.4 %feed_forward.1 = (bf16[2,256,1024]{2,1,0:T(8,128)(2,1)}, bf16[2,128,1024]{2,1,0:T(8,128)(2,1)}, bf16[2,128,1024]{2,1,0:T(8,128)(2,1)}, bf16[8,128,1024]{2,1,0:T...) custom-call(bf16[8,128,1024]{2,1,0:T(8,128)(2,1)} %bitcast.24, ...), custom_call_target="tpu_custom_call" | custom-call | tf_op jit(solution)/shard_map/feed_forward/pallas_call | solution.py:844
  216.6 118.5 %mixer_backward.1 = (bf16[2,128,1024]{2,1,0:T(8,128)(2,1)}, bf16[2,192,512]{2,1,0:T(8,128)(2,1)}, bf16[2,64,512]{2,1,0:T(8,128)(2,1)}, bf16[2,128,768]{2,1,0:T(8...) custom-call(bf16[8,128,1024]{2,1,0:T(8,128)(2,1)} %get-tuple-element, ...), custom_call_target="tpu_custom_call" | custom-call | tf_op jit(solution)/shard_map/mixer_backward/pallas_call | solution.py:844
  335.1 0.0 copy-start.1
  335.1 7.4 %place_gradients.1 = (bf16[16,256,128]{2,1,0:T(8,128)(2,1)}, f32[128,4096]{1,0:T(8,128)}, f32[128,24]{1,0:T(8,128)}, f32[192,1024]{1,0:T(8,128)}, f32[64,1024]{1...) custom-call(s32[16]{0:T(128)} %deal.1, bf16[2,128,1024]{2,1,0:T(8,128)(2,1)} %get-tuple-element.95.refs_0_, ...), custom_call_target="tpu_custom_call" | custom-call | tf_op jit(solution)/shard_map/place_gradients/pallas_call | solution.py:1503
  342.5 1.3 slice_bitcast_fusion
  343.8 1.3 slice_bitcast_fusion.1
  345.1 1.5 copy.31
  346.6 2.3 copy.33
  348.9 0.0 copy-done.1
  (2 shorter events, 0.0 us)
Async XLA Ops:
  0.6 3.6 %copy-start = (bf16[16,256,128]{2,1,0:T(8,128)(2,1)S(1)}, bf16[16,256,128]{2,1,0:T(8,128)(2,1)}, u32[]{:S(2)}) copy-start(bf16[16,256,128]{2,1,0:T(8,128)(2,1)} %param.18) | copy-start | bytes 3145732
  335.1 13.8 %copy-start.1 = (bf16[16,256,128]{2,1,0:T(8,128)(2,1)S(1)}, bf16[16,256,128]{2,1,0:T(8,128)(2,1)}, u32[]{:S(2)}) copy-start(bf16[16,256,128]{2,1,0:T(8,128)(2,1)} %param.18) | copy-start | bytes 3145732
where the time goes:
time: 353 us; the launch traced here: 349 us
  Pallas kernels  337 us (95%)
  local copies, waits for them, and re-layouts  8.12 us (2%)
    pallas_call x3, Pallas kernels, fused_call(): pl.pallas_call(wrapped, name=name, out_shape=tuple(outputs.values()), in_...  270 us
    pallas_call x1, Pallas kernels, start_transfers(): pl.pallas_call(start_kernel, name='deal_and_gather', out_shape=(jax.Shape...  59.2 us
    pallas_call x1, Pallas kernels, finish_stage(): pl.pallas_call(finish_kernel, name='place_gradients', out_shape=(shape(re...  7.38 us

commit v1 on v0

--- a/solution.py
+++ b/solution.py
@@ -1304,7 +1304,7 @@
     for step in sums[1:3]:
         step.start()
     tick = Ticker(reduce_steps(sums, partner))
-    tick.plan(2, 8)
+    tick.plan(0, 8)
     seq_len, width = k.normed_v.shape
     span = seq_len // 4
 
@@ -1320,17 +1320,17 @@
     grad_of(Z0, Z0 + XW, k.gz_v, 0)
     sums[3].start()
     mover.need(k.states_v)
-    tick.plan(14, 24)
+    tick.plan(10, 24)
     scan_backward(k.proj_v, k.segc_v, k.segr_v, k.par_v, k.spread_v, k.wide_v, k.y_v, k.states_v, k.ggated_v, k.gproj_v, k.gpar_v, k.gstate, tick)
     grad_of(X0, X0 + XW, k.xbc_v, 0)
     grad_of(B0, T0, k.xbc_v, XW)
     sums[4].start()
-    tick.plan(13, 20)
+    tick.plan(9, 20)
     mover.need(k.gattn_v, k.attn_v, k.lse_v, k.cosine_v, k.sine_v)
     attention_backward(k.proj_v, k.cosine_v, k.sine_v, k.segc_v, k.segr_v, k.attn_v, k.lse_v, k.gattn_v, k.gproj_v, k.gkv, tick)
     grad_of(Q0, B0, k.qkv_v, 0)
     sums[5].start()
-    tick.plan(6, 4)
+    tick.plan(4, 4)
     pair = (k.psend, k.precv)
     mover.need(k.w_in_v, k.rows_v, k.g_mid_v, k.gains_v, k.gffn_v)
     sent = []

time: 353 us -> 349 us (0.989)
  no operation moved by 1% of the time
where the time goes in v1:
time: 349 us; the launch traced here: 346 us
  Pallas kernels  334 us (96%)
  local copies, waits for them, and re-layouts  8.12 us (2%)
    pallas_call x3, Pallas kernels, fused_call(): pl.pallas_call(wrapped, name=name, out_shape=tuple(outputs.values()), in_...  267 us
    pallas_call x1, Pallas kernels, start_transfers(): pl.pallas_call(start_kernel, name='deal_and_gather', out_shape=(jax.Shape...  59.2 us
    pallas_call x1, Pallas kernels, finish_stage(): pl.pallas_call(finish_kernel, name='place_gradients', out_shape=(shape(re...  7.38 us

profile of v1, /device:TPU:9, one launch (start us, length us, event | category | flops | bytes accessed | tf_op | source)
XLA Modules:
  0.0 346.2 jit_solution(877479604157818502)
XLA Ops:
  0.6 0.0 copy-start
  0.7 0.7 compare_select_fusion
  1.4 0.1 pad.11.clone
  1.5 1.3 select_maximum_fusion.refs_5_
  2.8 1.4 maximum_maximum_fusion.beside
  4.2 0.0 copy-done
  4.2 1.6 gather_fusion
  5.9 59.2 %deal_and_gather.1 = (bf16[4,256,1024]{2,1,0:T(8,128)(2,1)}, bf16[8,128,2304]{2,1,0:T(8,128)(2,1)}) custom-call(bf16[16,256,128]{2,1,0:T(8,128)(2,1)} %gather_fusion, bf16[128,4096]{1,0:T(8,128)(2,1)} %in_proj.1, bf16[128,128]{1,0:T(8,128)(2,1)} %maximum_maximum_fusion.beside), custom_call_target="tpu_custom_call" | custom-call | tf_op jit(solution)/shard_map/deal_and_gather/pallas_call | solution.py:578
  65.1 85.1 %forward.1 = (bf16[1024,2304]{1,0:T(8,128)(2,1)}, bf16[1024,1024]{1,0:T(8,128)(2,1)}, f32[8,1024]{1,0:T(8,128)}, bf16[1024,256]{1,0:T(8,128)(2,1)}, f32[1024,128...) custom-call(bf16[1024,1024]{1,0:T(8,128)(2,1)} %bitcast.22, ...), custom_call_target="tpu_custom_call" | custom-call | tf_op jit(solution)/shard_map/forward/pallas_call | solution.py:844
  150.2 66.4 %feed_forward.1 = (bf16[2,256,1024]{2,1,0:T(8,128)(2,1)}, bf16[2,128,1024]{2,1,0:T(8,128)(2,1)}, bf16[2,128,1024]{2,1,0:T(8,128)(2,1)}, bf16[8,128,1024]{2,1,0:T...) custom-call(bf16[8,128,1024]{2,1,0:T(8,128)(2,1)} %bitcast.24, ...), custom_call_target="tpu_custom_call" | custom-call | tf_op jit(solution)/shard_map/feed_forward/pallas_call | solution.py:844
  216.6 115.6 %mixer_backward.1 = (bf16[2,128,1024]{2,1,0:T(8,128)(2,1)}, bf16[2,192,512]{2,1,0:T(8,128)(2,1)}, bf16[2,64,512]{2,1,0:T(8,128)(2,1)}, bf16[2,128,768]{2,1,0:T(8...) custom-call(bf16[8,128,1024]{2,1,0:T(8,128)(2,1)} %get-tuple-element, ...), custom_call_target="tpu_custom_call" | custom-call | tf_op jit(solution)/shard_map/mixer_backward/pallas_call | solution.py:844
  332.1 0.0 copy-start.1
  332.2 7.4 %place_gradients.1 = (bf16[16,256,128]{2,1,0:T(8,128)(2,1)}, f32[128,4096]{1,0:T(8,128)}, f32[128,24]{1,0:T(8,128)}, f32[192,1024]{1,0:T(8,128)}, f32[64,1024]{1...) custom-call(s32[16]{0:T(128)} %deal.1, bf16[2,128,1024]{2,1,0:T(8,128)(2,1)} %get-tuple-element.95.refs_0_, ...), custom_call_target="tpu_custom_call" | custom-call | tf_op jit(solution)/shard_map/place_gradients/pallas_call | solution.py:1503
  339.5 1.3 slice_bitcast_fusion
  340.8 1.3 slice_bitcast_fusion.1
  342.1 1.5 copy.31
  343.7 2.3 copy.33
  345.9 0.0 copy-done.1
  (2 shorter events, 0.0 us)
Async XLA Ops:
  0.6 3.6 %copy-start = (bf16[16,256,128]{2,1,0:T(8,128)(2,1)S(1)}, bf16[16,256,128]{2,1,0:T(8,128)(2,1)}, u32[]{:S(2)}) copy-start(bf16[16,256,128]{2,1,0:T(8,128)(2,1)} %param.18) | copy-start | bytes 3145732
  332.1 13.8 %copy-start.1 = (bf16[16,256,128]{2,1,0:T(8,128)(2,1)S(1)}, bf16[16,256,128]{2,1,0:T(8,128)(2,1)}, u32[]{:S(2)}) copy-start(bf16[16,256,128]{2,1,0:T(8,128)(2,1)} %param.18) | copy-start | bytes 3145732
